TPU v7x, 512 devices: a whole 4x4x16 slice. The times are simulated.
512 devices in a mesh: fsdp: 2 (over core), prompt: 16 (over y, z_lo), resp: 16 (over z_hi, x).
Axes of the slice: x: 4, y: 4, z: 16 (z_hi: 4, z_lo: 4; z = z_hi * 4 + z_lo), core: 2. Of those that a mesh axis runs over, the one named last changes fastest.
Arguments:
- prompt_query: bfloat16 [256, 128, 4096], P(('prompt', 'resp'), None, 'fsdp'), may hold values from -250 to 250
- prompt_key: bfloat16 [256, 128, 512], P(('prompt', 'resp'), None, 'fsdp'), may hold values from -6 to 6
- prompt_value: bfloat16 [256, 128, 512], P(('prompt', 'resp'), None, 'fsdp'), may hold values from -6 to 6
- prompt_adapter: bfloat16 [256, 128, 128], P(('prompt', 'resp')), may hold values from -6 to 6
- prompt_upstream: bfloat16 [256, 128, 4096], P(('prompt', 'resp'), None, 'fsdp'), may hold values from -6 to 6
- answer_query: bfloat16 [256, 256, 4096], P(('prompt', 'resp'), None, 'fsdp'), may hold values from -250 to 250
- answer_key: bfloat16 [256, 256, 512], P(('prompt', 'resp'), None, 'fsdp'), may hold values from -6 to 6
- answer_value: bfloat16 [256, 256, 512], P(('prompt', 'resp'), None, 'fsdp'), may hold values from -6 to 6
- answer_adapter: bfloat16 [256, 256, 128], P(('prompt', 'resp')), may hold values from -6 to 6
- answer_upstream: bfloat16 [256, 256, 4096], P(('prompt', 'resp'), None, 'fsdp'), may hold values from -6 to 6
- adapter_up: bfloat16 [2, 64, 512], P(None, None, 'fsdp'), may hold values from -0.75 to 0.75
- lengths: int32 [256, 2], P(('prompt', 'resp')), may hold values from 1 to 128, as said below
- pairing: int32 [16, 16], P('prompt'), may hold values from 0 to 15, each once within a row
Outputs:
- prompt_adapter_grad: float32 [256, 128, 128], P(('prompt', 'resp'))
- answer_adapter_grad: float32 [256, 256, 128], P(('prompt', 'resp'))
- adapter_up_grad: float32 [2, 64, 512], P(None, None, 'fsdp')
Inputs may be any that keep to these rules, and one draw needn't show every extreme that they name: Each row holds the lengths of one chosen and one rejected response; some length equals 128. `pairing`: each row is a permutation of the group's 16 indices.
All inputs are finite; a program needn't handle non-finite values.
Results may differ from a plain program's by a relative error of at most 0.02.
Values may be sent and summed in bfloat16 or wider, within the bound.
A program may use at most 64 MiB of HBM per device.

v0:
```python
import math

import jax
import jax.numpy as jnp
from jax import lax
from jax.sharding import PartitionSpec as P

HD = 128


exact_mode = lax.Precision.HIGHEST


def full_projection(base_rows, adapter_in, adapter_out):
    lifted = jnp.dot(adapter_in, adapter_out, preferred_element_type=jnp.float32)
    return (base_rows.astype(jnp.float32) + lifted).astype(jnp.bfloat16)


def attend_back(queries, key_rows, value_rows, upstream, visible):
    query_count = queries.shape[0]
    key_count = key_rows.shape[0]
    local_heads = key_rows.shape[1] // HD
    per_group = queries.shape[1] // HD // local_heads
    factor = 1.0 / math.sqrt(HD)
    query_heads = queries.reshape(query_count, local_heads, per_group, HD)
    key_heads = key_rows.reshape(key_count, local_heads, HD)
    value_heads = value_rows.reshape(key_count, local_heads, HD)
    grad_heads = upstream.reshape(query_count, local_heads, per_group, HD)
    scores = (
        jnp.einsum("rkgd,ckd->kgrc", query_heads, key_heads, preferred_element_type=jnp.float32)
        * factor
    )
    scores = jnp.where(visible, scores, -1e30)
    highest = jnp.max(scores, axis=-1, keepdims=True)
    weights = jnp.exp(scores - highest)
    probs_full = weights / jnp.sum(weights, axis=-1, keepdims=True)
    probs_low = probs_full.astype(jnp.bfloat16)
    output = jnp.einsum(
        "kgrc,ckd->rkgd", probs_low, value_heads, preferred_element_type=jnp.float32
    )
    row_delta = jnp.sum(grad_heads.astype(jnp.float32) * output, axis=-1)
    dprobs = jnp.einsum(
        "rkgd,ckd->kgrc", grad_heads, value_heads, preferred_element_type=jnp.float32
    )
    dscores = (probs_full * (dprobs - jnp.transpose(row_delta, (1, 2, 0))[..., None])).astype(
        jnp.bfloat16
    )
    key_grads = (
        jnp.einsum("kgrc,rkgd->ckd", dscores, query_heads, preferred_element_type=jnp.float32)
        * factor
    )
    value_grads = jnp.einsum(
        "kgrc,rkgd->ckd", probs_low, grad_heads, preferred_element_type=jnp.float32
    )
    return (
        key_grads.reshape(key_count, local_heads * HD),
        value_grads.reshape(key_count, local_heads * HD),
    )


def adapter_project(key_grad, value_grad, adapter_up):
    key_part = jnp.dot(key_grad, adapter_up[0].astype(jnp.float32).T, precision=exact_mode)
    value_part = jnp.dot(value_grad, adapter_up[1].astype(jnp.float32).T, precision=exact_mode)
    return jnp.concatenate([key_part, value_part], axis=1)


def adapter_outer(adapter_in, key_grad, value_grad):
    rank_width = adapter_in.shape[1] // 2
    inputs_wide = adapter_in.astype(jnp.float32)
    key_part = jnp.dot(inputs_wide[:, :rank_width].T, key_grad, precision=exact_mode)
    value_part = jnp.dot(inputs_wide[:, rank_width:].T, value_grad, precision=exact_mode)
    return jnp.stack([key_part, value_part])


def on_device(
    prompt_query,
    prompt_key,
    prompt_value,
    prompt_adapter,
    prompt_upstream,
    answer_query,
    answer_key,
    answer_value,
    answer_adapter,
    answer_upstream,
    adapter_up,
    lengths,
    pairing,
):
    rank_width = adapter_up.shape[1]
    prompt_len = prompt_query.shape[1]
    slot_count = answer_query.shape[1]
    most_len = slot_count // 2
    group_devices = lax.axis_size("resp")
    device_index = lax.axis_index("resp")
    owner_index = lax.dynamic_index_in_dim(pairing[0], device_index, keepdims=False)
    start_row = owner_index * prompt_len
    own_keys = full_projection(prompt_key[0], prompt_adapter[0, :, :rank_width], adapter_up[0])
    own_values = full_projection(prompt_value[0], prompt_adapter[0, :, rank_width:], adapter_up[1])
    slot_keys = full_projection(answer_key[0], answer_adapter[0, :, :rank_width], adapter_up[0])
    slot_values = full_projection(answer_value[0], answer_adapter[0, :, rank_width:], adapter_up[1])
    gathered_keys, gathered_values = (
        lax.all_gather(own_keys, "resp", axis=0, tiled=True),
        lax.all_gather(own_values, "resp", axis=0, tiled=True),
    )
    prefix_keys = lax.dynamic_slice_in_dim(gathered_keys, start_row, prompt_len, 0)
    prefix_values = lax.dynamic_slice_in_dim(gathered_values, start_row, prompt_len, 0)
    positions = jnp.arange(prompt_len, dtype=jnp.int32)
    causal = positions[None, :] <= positions[:, None]
    own_key_grad, own_value_grad = attend_back(
        prompt_query[0], own_keys, own_values, prompt_upstream[0], causal
    )
    slot_index = jnp.arange(slot_count, dtype=jnp.int32)
    part_index = slot_index // most_len
    place_index = slot_index % most_len
    live_mask = place_index < jnp.where(part_index == 0, lengths[0, 0], lengths[0, 1])
    answer_grad_in = answer_upstream[0] * live_mask[:, None].astype(jnp.bfloat16)
    same_part = (part_index[:, None] == part_index[None, :]) & (
        place_index[None, :] <= place_index[:, None]
    )
    answer_visible = jnp.concatenate(
        [jnp.ones((slot_count, prompt_len), dtype=bool), same_part], axis=1
    )
    key_rows = jnp.concatenate([prefix_keys, slot_keys], axis=0)
    value_rows = jnp.concatenate([prefix_values, slot_values], axis=0)
    all_key_grad, all_value_grad = attend_back(
        answer_query[0], key_rows, value_rows, answer_grad_in, answer_visible
    )
    prefix_key_grad = all_key_grad[:prompt_len]
    prefix_value_grad = all_value_grad[:prompt_len]
    slot_key_grad = all_key_grad[prompt_len:]
    slot_value_grad = all_value_grad[prompt_len:]
    answer_grad = adapter_project(slot_key_grad, slot_value_grad, adapter_up)
    grad_terms = adapter_outer(answer_adapter[0], slot_key_grad, slot_value_grad)
    key_width = prefix_key_grad.shape[1]
    zero_rows = jnp.zeros((group_devices * prompt_len, key_width), jnp.float32)
    send_keys = lax.dynamic_update_slice_in_dim(zero_rows, prefix_key_grad, start_row, 0)
    send_values = lax.dynamic_update_slice_in_dim(zero_rows, prefix_value_grad, start_row, 0)
    back_keys, back_values = (
        lax.psum_scatter(send_keys, "resp", scatter_dimension=0, tiled=True),
        lax.psum_scatter(send_values, "resp", scatter_dimension=0, tiled=True),
    )
    prompt_key_grad = own_key_grad + back_keys
    prompt_value_grad = own_value_grad + back_values
    prompt_grad = adapter_project(prompt_key_grad, prompt_value_grad, adapter_up)
    grad_terms = grad_terms + adapter_outer(prompt_adapter[0], prompt_key_grad, prompt_value_grad)
    prompt_grad, answer_grad = lax.psum((prompt_grad, answer_grad), "fsdp")
    summed = lax.psum(grad_terms, ("prompt", "resp"))
    prompt_total = lax.axis_size("prompt") * group_devices
    adapter_up_grad = summed / math.sqrt(prompt_total * (prompt_len + most_len))
    return (prompt_grad[None], answer_grad[None], adapter_up_grad)


def solution(mesh):
    in_specs = (
        P(("prompt", "resp"), None, "fsdp"),
        P(("prompt", "resp"), None, "fsdp"),
        P(("prompt", "resp"), None, "fsdp"),
        P(("prompt", "resp"), None, None),
        P(("prompt", "resp"), None, "fsdp"),
        P(("prompt", "resp"), None, "fsdp"),
        P(("prompt", "resp"), None, "fsdp"),
        P(("prompt", "resp"), None, "fsdp"),
        P(("prompt", "resp"), None, None),
        P(("prompt", "resp"), None, "fsdp"),
        P(None, None, "fsdp"),
        P(("prompt", "resp"), None),
        P("prompt", None),
    )
    out_specs = (
        P(("prompt", "resp"), None, None),
        P(("prompt", "resp"), None, None),
        P(None, None, "fsdp"),
    )
    return jax.shard_map(
        on_device, mesh=mesh, in_specs=in_specs, out_specs=out_specs, check_vma=False
    )
```

profile of v0, /device:TPU:1, one launch (start us, length us, event | category | flops | bytes accessed | tf_op | source)
XLA Modules:
  0.0 875.5 jit_solution(4624362860678173761)
XLA Ops:
  7.2 0.0 all-gather.3.cloned.1.call-start
  7.3 1.7 fusion.38
  9.0 0.0 all-gather.3.cloned.1.call-update
  9.0 0.0 all-gather.5.cloned.1.call-start
  9.1 1.7 fusion.39
  10.8 0.0 reduce-scatter.3.cloned.1.call-start
  10.9 1.2 fusion.102
  13.4 1.5 copy.67
  14.9 1.4 copy.64
  17.0 0.1 compare_and_fusion
  17.1 0.6 fusion.101
  17.7 1.8 compare_convert_fusion
  19.5 0.2 fusion.34
  19.7 0.2 fusion.35
  19.9 74.5 %all-gather.3.cloned.1.call-done = bf16[2048,256]{1,0:T(8,128)(2,1)} async-done(((bf16[128,256]{1,0:T(8,128)(2,1)}), bf16[2048,256]{1,0:T(8,128)(2,1)}) %all-gather.3.cloned.1.call-update) | async-done | bytes 1048592 | tf_op jit(solution)/shard_map/all_gather | solution.py:103
  94.4 0.8 constant_dynamic-slice_fusion.1
  95.2 0.1 reshape.110
  95.3 74.7 %all-gather.5.cloned.1.call-done = bf16[2048,256]{1,0:T(8,128)(2,1)} async-done(((bf16[128,256]{1,0:T(8,128)(2,1)}), bf16[2048,256]{1,0:T(8,128)(2,1)}) %all-gather.5.cloned.1.call-update) | async-done | bytes 1048592 | tf_op jit(solution)/shard_map/all_gather | solution.py:104
  170.0 0.8 constant_dynamic-slice_fusion
  170.9 0.2 copy.68
  171.1 4.8 fusion.103
  175.9 3.5 fusion.13
  179.4 1.3 fusion.14
  180.8 5.5 fusion.31
  186.3 1.6 broadcast_in_dim.49.clone.1
  187.9 0.7 constant_dynamic-update-slice_fusion.1
  188.6 0.0 reduce-scatter.5.cloned.1.call-start
  188.7 2.3 convolution_bitcast_fusion.2
  191.0 0.2 broadcast_in_dim.49.clone
  191.3 1.3 copy-done
  192.7 0.2 all-reduce.5.cloned.1.call-start
  192.9 0.7 copy.66
  193.7 0.3 copy.65
  194.0 0.5 fusion.108
  194.4 0.3 copy-done.12
  194.8 0.1 fusion.49
  194.9 0.4 copy.48
  195.3 0.1 copy.69
  195.5 0.5 copy.41
  195.9 2.1 fusion.23
  198.0 1.0 copy.32
  199.0 0.3 fusion.111
  199.4 1.7 fusion.37
  201.1 0.2 fusion.75
  201.4 0.2 fusion.68
  201.6 0.7 maximum_bitcast_fusion
  202.3 0.3 convolution_bitcast_fusion.6
  202.6 0.3 convolution_bitcast_fusion.5
  202.9 108.8 %reduce-scatter.3.cloned.1.call-done = f32[128,256]{0,1:T(8,128)} async-done(((f32[2048,256]{0,1:T(8,128)}), f32[128,256]{0,1:T(8,128)}) %reduce-scatter.3.cloned.1.call-update) | async-done | bytes 131088 | tf_op jit(solution)/shard_map/reduce_scatter | solution.py:140
  311.7 0.9 bitcast_add_fusion.1
  312.6 0.2 convolution_bitcast_fusion.4
  312.9 0.2 fusion.77
  313.0 124.1 %reduce-scatter.5.cloned.1.call-done = f32[128,256]{0,1:T(8,128)} async-done(((f32[2048,256]{0,1:T(8,128)}), f32[128,256]{0,1:T(8,128)}) %reduce-scatter.5.cloned.1.call-update) | async-done | bytes 131088 | tf_op jit(solution)/shard_map/reduce_scatter | solution.py:141
  437.1 0.9 bitcast_add_fusion
  438.0 0.3 convolution_bitcast_fusion.3
  438.4 0.7 maximum_add_fusion
  439.1 0.0 all-reduce.7.cloned.1.call-start
  439.1 0.2 fusion.70
  439.3 0.6 maximum_bitcast_fusion.1
  440.0 375.8 %all-reduce.5.cloned.1.call-done = f32[2,64,256]{2,1,0:T(8,128)} async-done(((f32[2,64,256]{2,1,0:T(8,128)}), f32[2,64,256]{2,1,0:T(8,128)}) %all-reduce.5.cloned.1.call-update) | async-done | bytes 131088 | tf_op jit(solution)/shard_map/psum | solution.py:148
  815.7 1.6 broadcast_multiply_fusion
  817.3 48.1 %all-reduce.7.cloned.1.call-done = (f32[1,128,128]{1,2,0:T(8,128)}, f32[1,256,128]{1,2,0:T(8,128)}) async-done(((f32[1,128,128]{1,2,0:T(8,128)}, f32[1,256,128]{1,2,0:T(8,128)}), (f32[1,128,128]{1,2,0:T(8,128)}, f32[1,256,128]{1,2,0:T(8,128)})) %all-reduce.7.cloned.1.call-update) | async-done | bytes 196624 | tf_op jit(solution)/shard_map/psum | solution.py:147
  865.4 1.7 copy.44
  867.1 1.6 copy.43
  (58 shorter events, 0.3 us)
Async XLA Ops:
  7.2 12.3 %copy-start.6 = (bf16[2,64,256]{2,1,0:T(8,128)(2,1)S(1)}, bf16[2,64,256]{2,1,0:T(8,128)(2,1)}, u32[]{:S(2)}) copy-start(bf16[2,64,256]{2,1,0:T(8,128)(2,1)} %param.23) | copy-start | bytes 196612
  7.2 7.7 copy-start.2
  7.2 9.9 %copy-start.21 = (s32[1,2]{1,0:T(1,128)S(1)}, s32[1,2]{1,0:T(1,128)}, u32[]{:S(2)}) copy-start(s32[1,2]{1,0:T(1,128)} %param.24) | copy-start | bytes 28
  7.2 12.3 %copy-start.17 = (bf16[1,256,256]{2,1,0:T(8,128)(2,1)S(1)}, bf16[1,256,256]{2,1,0:T(8,128)(2,1)}, u32[]{:S(2)}) copy-start(bf16[1,256,256]{2,1,0:T(8,128)(2,1)} %param.19) | copy-start | bytes 393220
  7.2 12.3 %copy-start.4 = (bf16[1,256,128]{2,1,0:T(8,128)(2,1)S(1)}, bf16[1,256,128]{2,1,0:T(8,128)(2,1)}, u32[]{:S(2)}) copy-start(bf16[1,256,128]{2,1,0:T(8,128)(2,1)} %param.21) | copy-start | bytes 196612
  7.2 12.4 %copy-start.18 = (bf16[1,256,256]{2,1,0:T(8,128)(2,1)S(1)}, bf16[1,256,256]{2,1,0:T(8,128)(2,1)}, u32[]{:S(2)}) copy-start(bf16[1,256,256]{2,1,0:T(8,128)(2,1)} %param.20) | copy-start | bytes 393220
  7.2 87.1 %all-gather.3.cloned.1.call-start = ((), (), s32[]{:S(2)}) async-start(), calls=%async_computation.2 | async-start | bytes 1114112 | tf_op jit(solution)/shard_map/all_gather | solution.py:103
  9.0 161.0 %all-gather.5.cloned.1.call-start = ((), (), s32[]{:S(2)}) async-start(), calls=%async_computation.3 | async-start | bytes 1114112 | tf_op jit(solution)/shard_map/all_gather | solution.py:104
  10.8 300.8 %reduce-scatter.3.cloned.1.call-start = ((), (), s32[]{:S(2)}) async-start(), calls=%async_computation.4 | async-start | bytes 2228224 | tf_op jit(solution)/shard_map/reduce_scatter | solution.py:140
  14.9 161.0 %copy-start.3 = (bf16[1,256,2048]{1,2,0:T(8,128)(2,1)}, bf16[1,256,2048]{1,2,0:T(8,128)(2,1)S(1)}, u32[]{:S(2)}) copy-start(bf16[1,256,2048]{1,2,0:T(8,128)(2,1)S(1)} %copy.67) | copy-start | bytes 3145732
  171.1 8.3 copy-start.16
  175.9 3.5 copy-start.1
  175.9 3.5 copy-start.19
  186.3 2.3 copy-start.14
  186.3 2.4 copy-start.20
  188.6 248.5 %reduce-scatter.5.cloned.1.call-start = ((), (), s32[]{:S(2)}) async-start(), calls=%async_computation.5 | async-start | bytes 2228224 | tf_op jit(solution)/shard_map/reduce_scatter | solution.py:141
  191.0 1.9 copy-start.8
  191.0 1.9 copy-start.9
  191.0 2.7 copy-start.10
  191.3 1.3 copy-start
  192.6 2.7 copy-start.11
  192.7 623.0 %all-reduce.5.cloned.1.call-start = ((), (), s32[]{:S(2)}) async-start(), calls=%async_computation.6 | async-start | bytes 262144 | tf_op jit(solution)/shard_map/psum | solution.py:148
  193.9 0.8 copy-start.12
  198.0 3.1 copy-start.15
  199.3 1.8 copy-start.7
  199.3 2.9 copy-start.5
  199.4 113.2 %copy-start.13 = (bf16[1,128,128]{2,1,0:T(8,128)(2,1)S(1)}, bf16[1,128,128]{2,1,0:T(8,128)(2,1)}, u32[]{:S(2)}) copy-start(bf16[1,128,128]{2,1,0:T(8,128)(2,1)} %param.16) | copy-start | bytes 98308
  439.1 426.4 %all-reduce.7.cloned.1.call-start = ((), (), s32[]{:S(2)}) async-start(), calls=%async_computation.7 | async-start | bytes 393216 | tf_op jit(solution)/shard_map/psum | solution.py:147
Sparse Core Ops, SparseCore 0:
  11.7 82.6 all-gather.2
  98.0 72.0 all-gather.4
  188.7 122.8 reduce-scatter.2
  316.2 120.8 reduce-scatter.4
  442.9 372.7 all-reduce.4
  819.3 46.0 all-reduce.6
where the time goes:
time: 876 us; the launch traced here: 875 us
  waiting for transfers between devices  806 us (92%)
  matrix products  24.3 us (3%)
  between operations  16.6 us (2%)
  local copies, waits for them, and re-layouts  15.9 us (2%)
  other arithmetic  12.2 us (1%)
    psum x1, waiting for transfers between devices, on_device(): summed = lax.psum(grad_terms, ('prompt', 'resp'))  376 us
    reduce_scatter x1, waiting for transfers between devices, on_device(): lax.psum_scatter(send_values, 'resp', scatter_dimension=0, tiled=True)  124 us
    reduce_scatter x1, waiting for transfers between devices, on_device(): lax.psum_scatter(send_keys, 'resp', scatter_dimension=0, tiled=True)  109 us
    all_gather x1, waiting for transfers between devices, on_device(): lax.all_gather(own_values, 'resp', axis=0, tiled=True)  74.7 us
    all_gather x1, waiting for transfers between devices, on_device(): lax.all_gather(own_keys, 'resp', axis=0, tiled=True)  74.5 us
    psum x1, waiting for transfers between devices, on_device(): prompt_grad, answer_grad = lax.psum((prompt_grad, answer_grad), 'fsdp')  48.1 us
  transfers between devices with their start and end apart: 6, of which 6 were waited for; matrix products, arithmetic and copies ran while one was open for 3% of the time, Pallas kernels for 0%

commit v1 on v0

v1 whole, which is shorter than its diff:
```python
import functools
import math

import jax
import jax.numpy as jnp
from jax import lax
from jax.experimental import pallas as pl
from jax.experimental.pallas import tpu as pltpu
from jax.sharding import PartitionSpec as P

MESH = pl.DeviceIdType.MESH
HD = 128
T = 128
N = 16
NT = (((1,), (1,)), ((), ()))
TN = (((0,), (0,)), ((), ()))
NN = (((1,), (0,)), ((), ()))
FACTOR = 1.0 / math.sqrt(HD)
EXP2_FACTOR = FACTOR * math.log2(math.e)


def mm(a, b, dims):
    return lax.dot_general(a, b, dims, preferred_element_type=jnp.float32)


def ready(ref, sem):
    pltpu.make_async_copy(ref, ref, sem).wait()


def backward_tile(keys, values, queries, grads, visible, live, prefix):
    scores = mm(keys, queries, NT)
    dprobs = mm(values, grads, NT)
    own = jnp.where(visible, scores[prefix:], -1e30)
    highest = jnp.max(own, axis=0, keepdims=True)
    if prefix:
        highest = jnp.maximum(highest, jnp.max(scores[:prefix], axis=0, keepdims=True))
        scores = jnp.concatenate([scores[:prefix], own], axis=0)
    else:
        scores = own
    weights = jnp.exp2((scores - highest) * EXP2_FACTOR)
    inverse = 1.0 / jnp.sum(weights, axis=0, keepdims=True)
    if live is not None:
        inverse = jnp.where(live, inverse, 0.0)
    probs = weights * inverse
    delta = jnp.sum(probs * dprobs, axis=0, keepdims=True)
    dscores = probs * (dprobs - delta)
    return probs.astype(jnp.bfloat16), dscores.astype(jnp.bfloat16)


def kernel(
    scale,
    pq_h, pk_h, pv_h, pa_h, pg_h, aq_h, ak_h, av_h, aa_h, ag_h, up_h, lens, pairing,
    prompt_out, answer_out, up_out,
    pq, pk, pv, pa, pg, aq, ak, av, aa, ag, up,
    wide_up, kv_own, kv_slot, kv_pre, mid1, mid2, amid1, amid2, a_pre,
    probs_s, dsc_s, dkv, own_proj, outer_acc,
    pre_send, bmid1, bmid2, pre_recv, pr_send, pr_recv, an_send, an_recv,
    gr_send, gr1, gr2_send, gr2, gr3_send, gr3,
    load_sem, send_sem, recv_sem,
):
    f = lax.axis_index("fsdp")
    p = lax.axis_index("prompt")
    r = lax.axis_index("resp")
    twin = 1 - f
    is_mid = lax.rem(r, 2) == f
    tile_at = r // 2

    loads = [
        pltpu.make_async_copy(src.at[0] if lead else src, dst, load_sem.at[i])
        for i, (src, dst, lead) in enumerate([
            (up_h, up, False), (pa_h, pa, True), (pk_h, pk, True), (pv_h, pv, True),
            (pq_h, pq, True), (pg_h, pg, True), (aa_h, aa, True), (ak_h, ak, True),
            (av_h, av, True), (aq_h, aq, True), (ag_h, ag, True),
        ])
    ]
    for load in loads:
        load.start()

    barrier = pltpu.get_barrier_semaphore()
    pl.semaphore_signal(barrier, inc=1, device_id={"fsdp": twin}, device_id_type=MESH)

    def greet(k, carry):
        pl.semaphore_signal(barrier, inc=1, device_id={"resp": lax.rem(r + k, N)}, device_id_type=MESH)
        pl.semaphore_signal(barrier, inc=1, device_id={"prompt": lax.rem(p + k, N)}, device_id_type=MESH)
        return carry

    lax.fori_loop(1, N, greet, 0)

    wide_up[...] = jnp.zeros_like(wide_up)
    for load in loads[:4]:
        load.wait()
    wide_up[0:64, 0:256] = up[0]
    wide_up[64:128, 256:512] = up[1]
    lifted = mm(pa[...], wide_up[...], NN)
    kv_own[0:128, :] = (pk[...].astype(jnp.float32) + lifted[:, 0:256]).astype(jnp.bfloat16)
    kv_own[128:256, :] = (pv[...].astype(jnp.float32) + lifted[:, 256:512]).astype(jnp.bfloat16)

    pl.semaphore_wait(barrier, 2 * (N - 1) + 1)

    def to(src, dst, lane, where):
        return pltpu.make_async_remote_copy(
            src_ref=src, dst_ref=dst, send_sem=send_sem.at[lane], recv_sem=recv_sem.at[lane],
            device_id=where, device_id_type=MESH,
        )

    def rows(index):
        return pl.ds(pl.multiple_of(index * 16, 16), 16)

    def to_mids(src_of, dst, lane):
        @pl.when(is_mid)
        def _():
            def step(k, carry):
                peer = lax.rem(r + 2 * k + 2, N)
                to(src_of(peer // 2), dst.at[r], lane, {"resp": peer}).start()
                return carry

            lax.fori_loop(0, 7, step, 0)
            dst[r] = src_of(tile_at)[...]

        @pl.when(jnp.logical_not(is_mid))
        def _():
            def step(k, carry):
                peer = lax.rem(r + 2 * k + 1, N)
                to(src_of(peer // 2), dst.at[r], lane, {"resp": peer}).start()
                return carry

            lax.fori_loop(0, 8, step, 0)

    def mids_sent(ref, lane):
        @pl.when(is_mid)
        def _():
            pltpu.make_async_copy(ref.at[pl.ds(0, 7)], ref.at[pl.ds(0, 7)], send_sem.at[lane]).wait()

        @pl.when(jnp.logical_not(is_mid))
        def _():
            pltpu.make_async_copy(ref.at[pl.ds(0, 8)], ref.at[pl.ds(0, 8)], send_sem.at[lane]).wait()

    def forward(k, carry):
        peer = lax.rem(r + k, N)
        to(kv_own.at[rows(peer)], mid1.at[r], 0, {"resp": peer}).start()
        return carry

    lax.fori_loop(1, N, forward, 0)
    mid1[r] = kv_own[rows(r), :]
    to_mids(lambda t: pa.at[rows(t)], amid1, 1)

    lane_at = lax.rem(lax.broadcasted_iota(jnp.int32, (T, 256), 1), T)
    visible = lax.broadcasted_iota(jnp.int32, (T, 256), 0) <= lane_at
    loads[4].wait()
    loads[5].wait()

    def own_head(h, carry):
        at = pl.multiple_of(h * HD, HD)
        keys = kv_own[0:128, pl.ds(at, HD)]
        values = kv_own[128:256, pl.ds(at, HD)]

        def heads(ref, g, count):
            return jnp.concatenate(
                [ref[:, pl.ds(pl.multiple_of(h * 1024 + (g + i) * HD, HD), HD)] for i in range(count)], axis=0
            )

        for g in range(0, 8, 2):
            probs, dscores = backward_tile(keys, values, heads(pq, g, 2), heads(pg, g, 2), visible, None, 0)
            probs_s[0, 0:128, g * HD:(g + 2) * HD] = probs
            dsc_s[0, 0:128, g * HD:(g + 2) * HD] = dscores
        dkv[0:128, pl.ds(at, HD)] = (mm(dsc_s[0, 0:128, :], heads(pq, 0, 8), NN) * FACTOR).astype(jnp.bfloat16)
        dkv[0:128, pl.ds(pl.multiple_of(256 + h * HD, HD), HD)] = mm(
            probs_s[0, 0:128, :], heads(pg, 0, 8), NN
        ).astype(jnp.bfloat16)
        return carry

    lax.fori_loop(0, 2, own_head, 0)

    ready(mid1.at[pl.ds(0, 15)], recv_sem.at[0])

    def onward(k, carry):
        peer = lax.rem(r + k, N)
        mid2[peer] = mid1[pairing[0, peer]]
        to(mid2.at[peer], kv_pre.at[rows(r)], 2, {"resp": peer}).start()
        return carry

    lax.fori_loop(1, N, onward, 0)
    kv_pre[rows(r), :] = mid1[pairing[0, r]]

    @pl.when(is_mid)
    def _():
        ready(amid1.at[pl.ds(0, 15)], recv_sem.at[1])

        def step(k, carry):
            peer = lax.rem(r + k, N)
            amid2[peer] = amid1[pairing[0, peer]]
            to(amid2.at[peer], a_pre.at[rows(tile_at)], 3, {"resp": peer}).start()
            return carry

        lax.fori_loop(1, N, step, 0)
        a_pre[rows(tile_at), :] = amid1[pairing[0, r]]

    own_proj[...] = mm(dkv[0:128, :], wide_up[...], NT)
    for load in loads[6:]:
        load.wait()
    lifted_slots = mm(aa[...], wide_up[...], NN)
    kv_slot[:, 0:256] = (ak[...].astype(jnp.float32) + lifted_slots[:, 0:256]).astype(jnp.bfloat16)
    kv_slot[:, 256:512] = (av[...].astype(jnp.float32) + lifted_slots[:, 256:512]).astype(jnp.bfloat16)
    outer_acc[...] = mm(pa[...], dkv[0:128, :], TN)

    ready(kv_pre.at[pl.ds(0, 240)], recv_sem.at[2])
    row_at = lax.rem(lax.broadcasted_iota(jnp.int32, (1, 256), 1), T)

    def slot_head(h, carry):
        at = pl.multiple_of(h * HD, HD)
        value_at = pl.multiple_of(256 + h * HD, HD)
        key_sum, value_sum = 0.0, 0.0
        for c in range(2):
            part = slice(c * T, (c + 1) * T)
            keys = jnp.concatenate([kv_pre[0:128, pl.ds(at, HD)], kv_slot[part, pl.ds(at, HD)]], axis=0)
            values = jnp.concatenate([kv_pre[128:256, pl.ds(at, HD)], kv_slot[part, pl.ds(value_at, HD)]], axis=0)
            live = row_at < lens[0, c]

            def heads(ref, g, count):
                return jnp.concatenate(
                    [ref[part, pl.ds(pl.multiple_of(h * 1024 + (g + i) * HD, HD), HD)] for i in range(count)], axis=0
                )

            for g in range(0, 8, 2):
                probs, dscores = backward_tile(keys, values, heads(aq, g, 2), heads(ag, g, 2), visible, live, T)
                probs_s[c, :, g * HD:(g + 2) * HD] = probs
                dsc_s[c, :, g * HD:(g + 2) * HD] = dscores
            key_grad = mm(dsc_s[c], heads(aq, 0, 8), NN) * FACTOR
            value_grad = mm(probs_s[c], heads(ag, 0, 8), NN)
            dkv[256 + c * T:256 + (c + 1) * T, pl.ds(at, HD)] = key_grad[T:].astype(jnp.bfloat16)
            dkv[256 + c * T:256 + (c + 1) * T, pl.ds(value_at, HD)] = value_grad[T:].astype(jnp.bfloat16)
            key_sum = key_sum + key_grad[:T]
            value_sum = value_sum + value_grad[:T]
        dkv[128:256, pl.ds(at, HD)] = key_sum.astype(jnp.bfloat16)
        dkv[128:256, pl.ds(value_at, HD)] = value_sum.astype(jnp.bfloat16)
        return carry

    lax.fori_loop(0, 2, slot_head, 0)

    pre_send[...] = mm(dkv[128:256, :], wide_up[...], NT).astype(jnp.bfloat16).reshape(8, 16, 128)
    to_mids(lambda t: pre_send.at[t], bmid1, 4)

    @pl.when(is_mid)
    def _():
        ready(a_pre.at[pl.ds(0, 112)], recv_sem.at[3])

    @pl.when(jnp.logical_not(is_mid))
    def _():
        ready(a_pre, recv_sem.at[3])

    outer = outer_acc[...] + mm(a_pre[...], dkv[128:256, :], TN) + mm(aa[...], dkv[256:512, :], TN)
    for b, (row, col) in enumerate([(0, 0), (0, 128), (64, 256), (64, 384)]):
        gr_send[4 * b:4 * b + 4] = outer[row:row + 64, col:col + 128].astype(jnp.bfloat16).reshape(4, 16, 128)

    def scatter(k, carry):
        peer = lax.rem(p + k, N)
        to(gr_send.at[peer], gr1.at[p], 5, {"prompt": peer}).start()
        return carry

    lax.fori_loop(1, N, scatter, 0)
    gr1[p] = gr_send[p]

    an_send[...] = mm(dkv[256:512, :], wide_up[...], NT).astype(jnp.bfloat16)
    to_twin = to(an_send, an_recv, 6, {"fsdp": twin})
    to_twin.start()

    @pl.when(is_mid)
    def _():
        ready(bmid1.at[pl.ds(0, 15)], recv_sem.at[4])

        def step(k, carry):
            peer = lax.rem(r + k, N)
            held = jnp.int32(0)
            for d in range(N):
                held = jnp.where(pairing[0, d] == peer, d, held)
            bmid2[peer] = bmid1[held]
            to(bmid2.at[peer], pre_recv.at[tile_at], 7, {"resp": peer}).start()
            return carry

        lax.fori_loop(1, N, step, 0)
        held = jnp.int32(0)
        for d in range(N):
            held = jnp.where(pairing[0, d] == r, d, held)
        pre_recv[tile_at] = bmid1[held]

    ready(gr1.at[pl.ds(0, 15)], recv_sem.at[5])
    part_sum = jnp.sum(gr1[...].astype(jnp.float32), axis=0).astype(jnp.bfloat16)
    gr2_send[...] = part_sum

    def spread(k, carry):
        peer = lax.rem(r + k, N)
        to(gr2_send, gr2.at[r], 8, {"resp": peer}).start()
        return carry

    lax.fori_loop(1, N, spread, 0)
    gr2[r] = part_sum

    to_twin.wait_recv()
    answer_out[0] = an_send[...].astype(jnp.float32) + an_recv[...].astype(jnp.float32)

    @pl.when(is_mid)
    def _():
        ready(pre_recv.at[pl.ds(0, 7)], recv_sem.at[7])

    @pl.when(jnp.logical_not(is_mid))
    def _():
        ready(pre_recv, recv_sem.at[7])

    pr_send[...] = (own_proj[...] + pre_recv[...].reshape(128, 128).astype(jnp.float32)).astype(jnp.bfloat16)
    prompt_twin = to(pr_send, pr_recv, 9, {"fsdp": twin})
    prompt_twin.start()

    ready(gr2.at[pl.ds(0, 15)], recv_sem.at[8])
    total = (jnp.sum(gr2[...].astype(jnp.float32), axis=0) * scale).astype(jnp.bfloat16)
    gr3_send[...] = total

    def collect(k, carry):
        peer = lax.rem(p + k, N)
        to(gr3_send, gr3.at[p], 10, {"prompt": peer}).start()
        return carry

    lax.fori_loop(1, N, collect, 0)
    gr3[p] = total

    prompt_twin.wait_recv()
    prompt_out[0] = pr_send[...].astype(jnp.float32) + pr_recv[...].astype(jnp.float32)

    ready(gr3.at[pl.ds(0, 15)], recv_sem.at[10])
    for b in range(4):
        up_out[b // 2, :, (b % 2) * 128:(b % 2) * 128 + 128] = (
            gr3[4 * b:4 * b + 4].reshape(64, 128).astype(jnp.float32)
        )

    ready(mid1.at[pl.ds(0, 15)], send_sem.at[0])
    mids_sent(amid1, 1)
    ready(mid2.at[pl.ds(0, 15)], send_sem.at[2])
    mids_sent(bmid1, 4)
    ready(gr_send.at[pl.ds(0, 15)], send_sem.at[5])
    to_twin.wait_send()
    ready(gr2.at[pl.ds(0, 15)], send_sem.at[8])
    prompt_twin.wait_send()
    ready(gr3.at[pl.ds(0, 15)], send_sem.at[10])

    @pl.when(is_mid)
    def _():
        ready(amid2.at[pl.ds(0, 15)], send_sem.at[3])
        ready(bmid2.at[pl.ds(0, 15)], send_sem.at[7])


def on_device(scale, *args):
    bf, f32 = jnp.bfloat16, jnp.float32
    hbm = pl.BlockSpec(memory_space=pl.ANY)
    vmem = pl.BlockSpec(memory_space=pltpu.VMEM)
    smem = pl.BlockSpec(memory_space=pltpu.SMEM)
    V = pltpu.VMEM
    return pl.pallas_call(
        functools.partial(kernel, scale),
        out_shape=(
            jax.ShapeDtypeStruct((1, 128, 128), f32),
            jax.ShapeDtypeStruct((1, 256, 128), f32),
            jax.ShapeDtypeStruct((2, 64, 256), f32),
        ),
        in_specs=[hbm] * 11 + [smem] * 2,
        out_specs=(vmem, vmem, vmem),
        scratch_shapes=[
            V((128, 2048), bf), V((128, 256), bf), V((128, 256), bf), V((128, 128), bf), V((128, 2048), bf),
            V((256, 2048), bf), V((256, 256), bf), V((256, 256), bf), V((256, 128), bf), V((256, 2048), bf),
            V((2, 64, 256), bf),
            V((128, 512), bf), V((256, 256), bf), V((256, 512), bf), V((256, 256), bf),
            V((16, 16, 256), bf), V((16, 16, 256), bf), V((16, 16, 128), bf), V((16, 16, 128), bf), V((128, 128), bf),
            V((2, 256, 1024), bf), V((2, 256, 1024), bf), V((512, 512), bf), V((128, 128), f32), V((128, 512), f32),
            V((8, 16, 128), bf), V((16, 16, 128), bf), V((16, 16, 128), bf), V((8, 16, 128), bf),
            V((128, 128), bf), V((128, 128), bf), V((256, 128), bf), V((256, 128), bf),
            V((16, 16, 128), bf), V((16, 16, 128), bf), V((16, 128), bf), V((16, 16, 128), bf),
            V((16, 128), bf), V((16, 16, 128), bf),
            pltpu.SemaphoreType.DMA((11,)), pltpu.SemaphoreType.DMA((11,)), pltpu.SemaphoreType.DMA((11,)),
        ],
        compiler_params=pltpu.CompilerParams(
            collective_id=0, has_side_effects=True, vmem_limit_bytes=48 * 1024 * 1024
        ),
        name="adapter_backward",
    )(*args)


def solution(mesh):
    rows = ("prompt", "resp")
    wide = P(rows, None, "fsdp")
    whole = P(rows, None, None)
    scale = 1.0 / math.sqrt(mesh.shape["prompt"] * mesh.shape["resp"] * 2 * T)
    return jax.shard_map(
        functools.partial(on_device, scale),
        mesh=mesh,
        in_specs=(
            wide, wide, wide, whole, wide, wide, wide, wide, whole, wide,
            P(None, None, "fsdp"), P(rows, None), P("prompt", None),
        ),
        out_specs=(whole, whole, P(None, None, "fsdp")),
        check_vma=False,
    )
```

time: 876 us -> 85.6 us (0.10)
  the two profiles are of different devices: /device:TPU:1 before, /device:TPU:6 now
where the time goes in v1:
time: 85.6 us; the launch traced here: 85 us
  Pallas kernels  70.6 us (82%)
  local copies, waits for them, and re-layouts  13.7 us (16%)
    pallas_call x1, Pallas kernels, on_device(): pl.pallas_call(functools.partial(kernel, scale), out_shape=(jax.ShapeDtyp...  70.6 us
    unnamed x29, local copies, waits for them, and re-layouts  13.7 us

profile of v1, /device:TPU:6, one launch (start us, length us, event | category | flops | bytes accessed | tf_op | source)
XLA Modules:
  0.0 85.0 jit_solution(2690429726734608012)
XLA Ops:
  0.6 0.0 copy-start
  0.6 1.2 %copy-done = bf16[1,256,2048]{2,1,0:T(8,128)(2,1)S(1)} copy-done((bf16[1,256,2048]{2,1,0:T(8,128)(2,1)S(1)}, bf16[1,256,2048]{2,1,0:T(8,128)(2,1)}, u32[]{:S(2)}) %copy-start) | copy-done | bytes 1048600
  1.9 0.0 copy-start.1
  1.9 1.2 %copy-done.1 = bf16[1,256,2048]{2,1,0:T(8,128)(2,1)S(1)} copy-done((bf16[1,256,2048]{2,1,0:T(8,128)(2,1)S(1)}, bf16[1,256,2048]{2,1,0:T(8,128)(2,1)}, u32[]{:S(2)}) %copy-start.1) | copy-done | bytes 1048600
  3.1 0.0 copy-start.2
  3.1 1.0 %copy-done.2 = bf16[1,128,2048]{2,1,0:T(8,128)(2,1)S(1)} copy-done((bf16[1,128,2048]{2,1,0:T(8,128)(2,1)S(1)}, bf16[1,128,2048]{2,1,0:T(8,128)(2,1)}, u32[]{:S(2)}) %copy-start.2) | copy-done | bytes 524312
  4.1 0.0 copy-start.3
  4.1 1.0 %copy-done.3 = bf16[1,128,2048]{2,1,0:T(8,128)(2,1)S(1)} copy-done((bf16[1,128,2048]{2,1,0:T(8,128)(2,1)S(1)}, bf16[1,128,2048]{2,1,0:T(8,128)(2,1)}, u32[]{:S(2)}) %copy-start.3) | copy-done | bytes 524312
  5.2 0.0 copy-start.4
  5.2 0.9 %copy-done.4 = bf16[1,256,256]{2,1,0:T(8,128)(2,1)S(1)} copy-done((bf16[1,256,256]{2,1,0:T(8,128)(2,1)S(1)}, bf16[1,256,256]{2,1,0:T(8,128)(2,1)}, u32[]{:S(2)}) %copy-start.4) | copy-done | bytes 131096
  6.1 0.0 copy-start.5
  6.1 0.9 %copy-done.5 = bf16[1,256,256]{2,1,0:T(8,128)(2,1)S(1)} copy-done((bf16[1,256,256]{2,1,0:T(8,128)(2,1)S(1)}, bf16[1,256,256]{2,1,0:T(8,128)(2,1)}, u32[]{:S(2)}) %copy-start.5) | copy-done | bytes 131096
  7.0 0.0 copy-start.6
  7.0 0.8 copy-done.6
  7.8 0.0 copy-start.7
  7.8 0.8 copy-done.7
  8.7 0.0 copy-start.8
  8.7 0.8 copy-done.8
  9.5 0.0 copy-start.9
  9.5 0.8 copy-done.9
  10.3 0.0 copy-start.10
  10.3 0.8 copy-done.10
  11.1 0.0 copy-start.11
  11.1 0.7 copy-done.11
  11.8 0.0 copy-start.12
  11.8 0.7 copy-done.12
  12.4 70.6 %adapter_backward.1 = (f32[1,128,128]{2,1,0:T(8,128)S(1)}, f32[1,256,128]{2,1,0:T(8,128)S(1)}, f32[2,64,256]{2,1,0:T(8,128)S(1)}) custom-call(bf16[1,128,2048]{2,1,0:T(8,128)(2,1)S(1)} %copy-done.2, bf16[1,128,256]{2,1,0:T(8,128)(2,1)S(1)} %copy-done.6, bf16[1,128,256]{2,1,0:T(8,128)(2,1)S(1)} %copy-done.7, bf16[1,128,128]{2,1,0:T(8,128)(2,1)S(1)} %copy-done.10, ...), custom_call_target="tpu_custom_call" | custom-call | tf_op jit(solution)/shard_map/adapter_backward/pallas_call | solution.py:356
  83.0 0.6 copy.19
  83.7 0.7 copy.20
  84.3 0.7 copy.21
Async XLA Ops:
  0.6 1.2 %copy-start = (bf16[1,256,2048]{2,1,0:T(8,128)(2,1)S(1)}, bf16[1,256,2048]{2,1,0:T(8,128)(2,1)}, u32[]{:S(2)}) copy-start(bf16[1,256,2048]{2,1,0:T(8,128)(2,1)} %aq_h.1) | copy-start | bytes 3145732
  1.9 1.2 %copy-start.1 = (bf16[1,256,2048]{2,1,0:T(8,128)(2,1)S(1)}, bf16[1,256,2048]{2,1,0:T(8,128)(2,1)}, u32[]{:S(2)}) copy-start(bf16[1,256,2048]{2,1,0:T(8,128)(2,1)} %ag_h.1) | copy-start | bytes 3145732
  3.1 1.0 %copy-start.2 = (bf16[1,128,2048]{2,1,0:T(8,128)(2,1)S(1)}, bf16[1,128,2048]{2,1,0:T(8,128)(2,1)}, u32[]{:S(2)}) copy-start(bf16[1,128,2048]{2,1,0:T(8,128)(2,1)} %pq_h.1) | copy-start | bytes 1572868
  4.1 1.0 %copy-start.3 = (bf16[1,128,2048]{2,1,0:T(8,128)(2,1)S(1)}, bf16[1,128,2048]{2,1,0:T(8,128)(2,1)}, u32[]{:S(2)}) copy-start(bf16[1,128,2048]{2,1,0:T(8,128)(2,1)} %pg_h.1) | copy-start | bytes 1572868
  5.2 0.9 %copy-start.4 = (bf16[1,256,256]{2,1,0:T(8,128)(2,1)S(1)}, bf16[1,256,256]{2,1,0:T(8,128)(2,1)}, u32[]{:S(2)}) copy-start(bf16[1,256,256]{2,1,0:T(8,128)(2,1)} %ak_h.1) | copy-start | bytes 393220
  6.1 0.9 %copy-start.5 = (bf16[1,256,256]{2,1,0:T(8,128)(2,1)S(1)}, bf16[1,256,256]{2,1,0:T(8,128)(2,1)}, u32[]{:S(2)}) copy-start(bf16[1,256,256]{2,1,0:T(8,128)(2,1)} %av_h.1) | copy-start | bytes 393220
  7.0 0.8 copy-start.6
  7.8 0.8 copy-start.7
  8.7 0.8 copy-start.8
  9.5 0.8 copy-start.9
  10.3 0.8 copy-start.10
  11.1 0.7 copy-start.11
  11.8 0.7 copy-start.12

commit v2 on v1

v2 whole, which is shorter than its diff:
```python
import functools
import math

import jax
import jax.numpy as jnp
from jax import lax
from jax.experimental import pallas as pl
from jax.experimental.pallas import tpu as pltpu
from jax.sharding import PartitionSpec as P

MESH = pl.DeviceIdType.MESH
HD = 128
T = 128
N = 16
NT = (((1,), (1,)), ((), ()))
TN = (((0,), (0,)), ((), ()))
NN = (((1,), (0,)), ((), ()))
FACTOR = 1.0 / math.sqrt(HD)
EXP2_FACTOR = FACTOR * math.log2(math.e)
RESP_ORDER = (10, 9, 11, 8, 6, 14, 5, 7, 13, 15, 4, 12, 2, 1, 3)
PLANE_ORDER = (10, 9, 11, 6, 14, 8, 2, 5, 7, 13, 15, 4, 12, 1, 3)
RING_ORDER = (8, 7, 9, 6, 10, 5, 11, 4, 12, 3, 13, 2, 14, 1, 15)


def mm(a, b, dims):
    return lax.dot_general(a, b, dims, preferred_element_type=jnp.float32)


def ready(ref, sem):
    pltpu.make_async_copy(ref, ref, sem).wait()


def backward_tile(keys, values, queries, grads, visible, live, prefix):
    scores = mm(keys, queries, NT)
    dprobs = mm(values, grads, NT)
    own = jnp.where(visible, scores[prefix:], -1e30)
    highest = jnp.max(own, axis=0, keepdims=True)
    if prefix:
        highest = jnp.maximum(highest, jnp.max(scores[:prefix], axis=0, keepdims=True))
        scores = jnp.concatenate([scores[:prefix], own], axis=0)
    else:
        scores = own
    weights = jnp.exp2((scores - highest) * EXP2_FACTOR)
    inverse = 1.0 / jnp.sum(weights, axis=0, keepdims=True)
    if live is not None:
        inverse = jnp.where(live, inverse, 0.0)
    probs = weights * inverse
    delta = jnp.sum(probs * dprobs, axis=0, keepdims=True)
    dscores = probs * (dprobs - delta)
    return probs.astype(jnp.bfloat16), dscores.astype(jnp.bfloat16)


def kernel(
    scale,
    pq_h, pk_h, pv_h, pa_h, pg_h, aq_h, ak_h, av_h, aa_h, ag_h, up_h, lens_h, pairing_h,
    prompt_out, answer_out, up_out,
    pq, pk, pv, pa, pg, aq, ak, av, aa, ag, up, lens, pairing,
    wide_up, kv_own, kv_slot, kv_pre, mid1, mid2, amid1, amid2, a_pre,
    probs_s, dsc_s, dkv, own_proj, outer_acc,
    own_half, own_twin, pre_part, pre_twin, pre_half, pre_x, pre_z, pre_pick, pre_home, done_half, done_twin,
    an_send, an_recv, gr_send, gr1, gr2_send, gr2, gr3_send, gr3,
    load_sem, send_sem, recv_sem,
):
    f = lax.axis_index("fsdp")
    p = lax.axis_index("prompt")
    r = lax.axis_index("resp")
    twin = {"fsdp": 1 - f}
    x, z_hi = lax.rem(r, 4), r // 4
    y, z_lo = p // 4, lax.rem(p, 4)
    is_mid = lax.rem(r, 4) == 2 * f
    plane = y * 4 + x
    ring = z_hi * 4 + z_lo

    def in_plane(at):
        return {"prompt": (at // 4) * 4 + z_lo, "resp": z_hi * 4 + lax.rem(at, 4)}

    def in_ring(at):
        return {"prompt": y * 4 + lax.rem(at, 4), "resp": (at // 4) * 4 + x}

    def along_x(k):
        return z_hi * 4 + lax.rem(x + k, 4)

    def along_z(k):
        return lax.rem(z_hi + k, 4) * 4 + x

    barrier = pltpu.get_barrier_semaphore()

    def greet(where):
        pl.semaphore_signal(barrier, inc=1, device_id=where, device_id_type=MESH)

    for k in RESP_ORDER:
        greet({"resp": lax.rem(r + k, N)})

    loads = [
        pltpu.make_async_copy(src.at[0] if lead else src, dst, load_sem.at[i])
        for i, (src, dst, lead) in enumerate([
            (up_h, up, False), (pa_h, pa, True), (pk_h, pk, True), (pv_h, pv, True),
            (pq_h, pq, True), (pg_h, pg, True), (aa_h, aa, True), (ak_h, ak, True),
            (av_h, av, True), (aq_h, aq, True), (ag_h, ag, True), (lens_h, lens, False), (pairing_h, pairing, False),
        ])
    ]
    for load in loads:
        load.start()

    greet(twin)
    for k in range(4, N):
        greet({"prompt": (lax.rem(y + k // 4, 4)) * 4 + z_lo, "resp": along_x(k % 4)})
    for k in range(4, N):
        greet({"prompt": y * 4 + lax.rem(z_lo + k // 4, 4), "resp": along_z(k % 4)})

    wide_up[...] = jnp.zeros_like(wide_up)
    for load in loads[:4]:
        load.wait()
    wide_up[0:64, 0:256] = up[0]
    wide_up[64:128, 256:512] = up[1]
    lifted = mm(pa[...], wide_up[...], NN)
    kv_own[0:128, :] = (pk[...].astype(jnp.float32) + lifted[:, 0:256]).astype(jnp.bfloat16)
    kv_own[128:256, :] = (pv[...].astype(jnp.float32) + lifted[:, 256:512]).astype(jnp.bfloat16)

    pl.semaphore_wait(barrier, 40)

    def to(src, dst, lane, where):
        return pltpu.make_async_remote_copy(
            src_ref=src, dst_ref=dst, send_sem=send_sem.at[lane], recv_sem=recv_sem.at[lane],
            device_id=where, device_id_type=MESH,
        )

    def rows(index, size=16):
        return pl.ds(pl.multiple_of(index * size, size), size)

    for k in RESP_ORDER:
        peer = lax.rem(r + k, N)
        to(kv_own.at[rows(peer)], mid1.at[r], 0, {"resp": peer}).start()
    mid1[r] = kv_own[rows(r), :]
    for i in range(4):
        member = 4 * i + 2 * f

        @pl.when(member != r)
        def _():
            to(pa.at[rows(4 * f + i)], amid1.at[r], 1, {"resp": member}).start()

    @pl.when(is_mid)
    def _():
        amid1[r] = pa[rows(4 * f + z_hi), :]

    lane_at = lax.rem(lax.broadcasted_iota(jnp.int32, (T, 256), 1), T)
    visible = lax.broadcasted_iota(jnp.int32, (T, 256), 0) <= lane_at
    loads[4].wait()
    loads[5].wait()

    def own_head(h, carry):
        at = pl.multiple_of(h * HD, HD)
        keys = kv_own[0:128, pl.ds(at, HD)]
        values = kv_own[128:256, pl.ds(at, HD)]

        def heads(ref, g, count):
            return jnp.concatenate(
                [ref[:, pl.ds(pl.multiple_of(h * 1024 + (g + i) * HD, HD), HD)] for i in range(count)], axis=0
            )

        for g in range(0, 8, 2):
            probs, dscores = backward_tile(keys, values, heads(pq, g, 2), heads(pg, g, 2), visible, None, 0)
            probs_s[0, 0:128, g * HD:(g + 2) * HD] = probs
            dsc_s[0, 0:128, g * HD:(g + 2) * HD] = dscores
        dkv[0:128, pl.ds(at, HD)] = (mm(dsc_s[0, 0:128, :], heads(pq, 0, 8), NN) * FACTOR).astype(jnp.bfloat16)
        dkv[0:128, pl.ds(pl.multiple_of(256 + h * HD, HD), HD)] = mm(
            probs_s[0, 0:128, :], heads(pg, 0, 8), NN
        ).astype(jnp.bfloat16)
        return carry

    lax.fori_loop(0, 2, own_head, 0)

    loads[12].wait()
    ready(mid1.at[pl.ds(0, 15)], recv_sem.at[0])
    for k in RESP_ORDER:
        peer = lax.rem(r + k, N)
        mid2[peer] = mid1[pairing[0, peer]]
        to(mid2.at[peer], kv_pre.at[rows(r)], 2, {"resp": peer}).start()
    kv_pre[rows(r), :] = mid1[pairing[0, r]]

    @pl.when(is_mid)
    def _():
        ready(amid1.at[pl.ds(0, 15)], recv_sem.at[1])
        for k in RESP_ORDER:
            peer = lax.rem(r + k, N)
            amid2[peer] = amid1[pairing[0, peer]]
            to(amid2.at[peer], a_pre.at[rows(4 * f + z_hi)], 3, {"resp": peer}).start()
        a_pre[rows(4 * f + z_hi), :] = amid1[pairing[0, r]]

    own_proj[...] = mm(dkv[0:128, :], wide_up[...], NT)
    own_half[...] = own_proj[rows(1 - f, 64), :].astype(jnp.bfloat16)
    own_copy = to(own_half, own_twin, 4, twin)
    own_copy.start()
    for load in loads[6:12]:
        load.wait()
    lifted_slots = mm(aa[...], wide_up[...], NN)
    kv_slot[:, 0:256] = (ak[...].astype(jnp.float32) + lifted_slots[:, 0:256]).astype(jnp.bfloat16)
    kv_slot[:, 256:512] = (av[...].astype(jnp.float32) + lifted_slots[:, 256:512]).astype(jnp.bfloat16)
    outer_acc[...] = mm(pa[...], dkv[0:128, :], TN)

    ready(kv_pre.at[pl.ds(0, 240)], recv_sem.at[2])
    row_at = lax.rem(lax.broadcasted_iota(jnp.int32, (1, 256), 1), T)

    def slot_head(h, carry):
        at = pl.multiple_of(h * HD, HD)
        value_at = pl.multiple_of(256 + h * HD, HD)
        key_sum, value_sum = 0.0, 0.0
        for c in range(2):
            part = slice(c * T, (c + 1) * T)
            keys = jnp.concatenate([kv_pre[0:128, pl.ds(at, HD)], kv_slot[part, pl.ds(at, HD)]], axis=0)
            values = jnp.concatenate([kv_pre[128:256, pl.ds(at, HD)], kv_slot[part, pl.ds(value_at, HD)]], axis=0)
            live = row_at < lens[0, c]

            def heads(ref, g, count):
                return jnp.concatenate(
                    [ref[part, pl.ds(pl.multiple_of(h * 1024 + (g + i) * HD, HD), HD)] for i in range(count)], axis=0
                )

            for g in range(0, 8, 2):
                probs, dscores = backward_tile(keys, values, heads(aq, g, 2), heads(ag, g, 2), visible, live, T)
                probs_s[c, :, g * HD:(g + 2) * HD] = probs
                dsc_s[c, :, g * HD:(g + 2) * HD] = dscores
            key_grad = mm(dsc_s[c], heads(aq, 0, 8), NN) * FACTOR
            value_grad = mm(probs_s[c], heads(ag, 0, 8), NN)
            dkv[256 + c * T:256 + (c + 1) * T, pl.ds(at, HD)] = key_grad[T:].astype(jnp.bfloat16)
            dkv[256 + c * T:256 + (c + 1) * T, pl.ds(value_at, HD)] = value_grad[T:].astype(jnp.bfloat16)
            key_sum = key_sum + key_grad[:T]
            value_sum = value_sum + value_grad[:T]
        dkv[128:256, pl.ds(at, HD)] = key_sum.astype(jnp.bfloat16)
        dkv[128:256, pl.ds(value_at, HD)] = value_sum.astype(jnp.bfloat16)
        return carry

    @pl.when(is_mid)
    def _():
        ready(a_pre.at[pl.ds(0, 48)], recv_sem.at[3])

    @pl.when(jnp.logical_not(is_mid))
    def _():
        ready(a_pre.at[pl.ds(0, 64)], recv_sem.at[3])

    a_copy = to(a_pre.at[rows(f, 64)], a_pre.at[rows(f, 64)], 5, twin)
    a_copy.start()

    lax.fori_loop(0, 2, slot_head, 0)

    pre_part[...] = mm(dkv[128:256, :], wide_up[...], NT)
    pre_half[0] = pre_part[rows(1 - f, 64), :].astype(jnp.bfloat16)
    pre_copy = to(pre_half.at[0], pre_twin, 6, twin)
    pre_copy.start()

    ready(a_pre.at[pl.ds(0, 64)], recv_sem.at[5])
    outer = outer_acc[...] + mm(a_pre[...], dkv[128:256, :], TN) + mm(aa[...], dkv[256:512, :], TN)
    for b, (row, col) in enumerate([(0, 0), (0, 128), (64, 256), (64, 384)]):
        gr_send[4 * b:4 * b + 4] = outer[row:row + 64, col:col + 128].astype(jnp.bfloat16).reshape(4, 16, 128)
    for k in PLANE_ORDER:
        peer = (lax.rem(y + k // 4, 4)) * 4 + lax.rem(x + k % 4, 4)
        to(gr_send.at[peer], gr1.at[plane], 7, in_plane(peer)).start()
    gr1[plane] = gr_send[plane]

    ready(pre_twin, recv_sem.at[6])
    pre_half[1] = (pre_part[rows(f, 64), :] + pre_twin[...].astype(jnp.float32)).astype(jnp.bfloat16)
    for k in (2, 1, 3):
        peer_x = lax.rem(x + k, 4)
        to(pre_half.at[1, rows(peer_x)], pre_x.at[x], 8, {"resp": z_hi * 4 + peer_x}).start()
    pre_x[x] = pre_half[1, rows(x), :]

    an_send[...] = mm(dkv[256:512, :], wide_up[...], NT).astype(jnp.bfloat16)
    to_twin = to(an_send, an_recv, 9, twin)
    to_twin.start()

    ready(pre_x.at[pl.ds(0, 3)], recv_sem.at[8])
    for k in (2, 1, 3):
        to(pre_x, pre_z.at[z_hi], 10, {"resp": along_z(k)}).start()
    pre_z[z_hi] = pre_x[...]

    ready(gr1.at[pl.ds(0, 15)], recv_sem.at[7])
    part_sum = jnp.sum(gr1[...].astype(jnp.float32), axis=0).astype(jnp.bfloat16)
    gr2_send[...] = part_sum
    for k in RING_ORDER:
        to(gr2_send, gr2.at[ring], 11, in_ring(lax.rem(ring + k, N))).start()
    gr2[ring] = part_sum

    ready(an_recv, recv_sem.at[9])
    answer_out[0] = an_send[...].astype(jnp.float32) + an_recv[...].astype(jnp.float32)

    def responder(owner):
        held = jnp.int32(0)
        for d in range(N):
            held = jnp.where(pairing[0, d] == owner, d, held)
        return held

    sources = [responder(along_x(k)) for k in range(4)]
    ready(own_twin, recv_sem.at[4])
    ready(pre_z.at[pl.ds(0, 3)], recv_sem.at[10])
    for k in (2, 1, 3):
        pre_pick[k] = pre_z[sources[k] // 4, lax.rem(sources[k], 4)]
        to(pre_pick.at[k], pre_home.at[x], 12, {"resp": along_x(k)}).start()
    pre_home[x] = pre_z[sources[0] // 4, lax.rem(sources[0], 4)]

    ready(gr2.at[pl.ds(0, 15)], recv_sem.at[11])
    total = (jnp.sum(gr2[...].astype(jnp.float32), axis=0) * scale).astype(jnp.bfloat16)
    gr3_send[...] = total
    for k in PLANE_ORDER:
        peer = (lax.rem(y + k // 4, 4)) * 4 + lax.rem(x + k % 4, 4)
        to(gr3_send, gr3.at[plane], 13, in_plane(peer)).start()
    gr3[plane] = total

    ready(pre_home.at[pl.ds(0, 3)], recv_sem.at[12])
    done = (
        own_proj[rows(f, 64), :]
        + own_twin[...].astype(jnp.float32)
        + pre_home[...].reshape(64, 128).astype(jnp.float32)
    )
    done_half[...] = done
    done_copy = to(done_half, done_twin, 14, twin)
    done_copy.start()
    prompt_out[0, rows(f, 64), :] = done
    ready(done_twin, recv_sem.at[14])
    prompt_out[0, rows(1 - f, 64), :] = done_twin[...]

    ready(gr3.at[pl.ds(0, 15)], recv_sem.at[13])
    for b in range(4):
        up_out[b // 2, :, (b % 2) * 128:(b % 2) * 128 + 128] = (
            gr3[4 * b:4 * b + 4].reshape(64, 128).astype(jnp.float32)
        )

    ready(mid1.at[pl.ds(0, 15)], send_sem.at[0])
    ready(mid2.at[pl.ds(0, 15)], send_sem.at[2])
    own_copy.wait_send()
    a_copy.wait_send()
    pre_copy.wait_send()
    ready(gr_send.at[pl.ds(0, 15)], send_sem.at[7])
    ready(pre_x.at[pl.ds(0, 3)], send_sem.at[8])
    to_twin.wait_send()
    ready(pre_z.at[pl.ds(0, 3)], send_sem.at[10])
    ready(gr2.at[pl.ds(0, 15)], send_sem.at[11])
    ready(pre_pick.at[pl.ds(0, 3)], send_sem.at[12])
    ready(gr3.at[pl.ds(0, 15)], send_sem.at[13])
    done_copy.wait_send()

    @pl.when(is_mid)
    def _():
        ready(amid1.at[pl.ds(0, 3)], send_sem.at[1])
        ready(amid2.at[pl.ds(0, 15)], send_sem.at[3])

    @pl.when(jnp.logical_not(is_mid))
    def _():
        ready(amid1.at[pl.ds(0, 4)], send_sem.at[1])


def on_device(scale, *args):
    bf, f32 = jnp.bfloat16, jnp.float32
    hbm = pl.BlockSpec(memory_space=pltpu.HBM)
    vmem = pl.BlockSpec(memory_space=pltpu.VMEM)
    V = pltpu.VMEM
    return pl.pallas_call(
        functools.partial(kernel, scale),
        out_shape=(
            jax.ShapeDtypeStruct((1, 128, 128), f32),
            jax.ShapeDtypeStruct((1, 256, 128), f32),
            jax.ShapeDtypeStruct((2, 64, 256), f32),
        ),
        in_specs=[hbm] * 13,
        out_specs=(vmem, vmem, vmem),
        scratch_shapes=[
            V((128, 2048), bf), V((128, 256), bf), V((128, 256), bf), V((128, 128), bf), V((128, 2048), bf),
            V((256, 2048), bf), V((256, 256), bf), V((256, 256), bf), V((256, 128), bf), V((256, 2048), bf),
            V((2, 64, 256), bf), pltpu.SMEM((1, 2), jnp.int32), pltpu.SMEM((1, 16), jnp.int32),
            V((128, 512), bf), V((256, 256), bf), V((256, 512), bf), V((256, 256), bf),
            V((16, 16, 256), bf), V((16, 16, 256), bf), V((16, 16, 128), bf), V((16, 16, 128), bf), V((128, 128), bf),
            V((2, 256, 1024), bf), V((2, 256, 1024), bf), V((512, 512), bf), V((128, 128), f32), V((128, 512), f32),
            V((64, 128), bf), V((64, 128), bf), V((128, 128), f32), V((64, 128), bf), V((2, 64, 128), bf),
            V((4, 16, 128), bf), V((4, 4, 16, 128), bf), V((4, 16, 128), bf), V((4, 16, 128), bf),
            V((64, 128), f32), V((64, 128), f32),
            V((256, 128), bf), V((256, 128), bf),
            V((16, 16, 128), bf), V((16, 16, 128), bf), V((16, 128), bf), V((16, 16, 128), bf),
            V((16, 128), bf), V((16, 16, 128), bf),
            pltpu.SemaphoreType.DMA((13,)), pltpu.SemaphoreType.DMA((15,)), pltpu.SemaphoreType.DMA((15,)),
        ],
        compiler_params=pltpu.CompilerParams(
            collective_id=0, has_side_effects=True, vmem_limit_bytes=60 * 1024 * 1024
        ),
        name="adapter_backward",
    )(*args)


def solution(mesh):
    rows = ("prompt", "resp")
    wide = P(rows, None, "fsdp")
    whole = P(rows, None, None)
    scale = 1.0 / math.sqrt(mesh.shape["prompt"] * mesh.shape["resp"] * 2 * T)
    return jax.shard_map(
        functools.partial(on_device, scale),
        mesh=mesh,
        in_specs=(
            wide, wide, wide, whole, wide, wide, wide, wide, whole, wide,
            P(None, None, "fsdp"), P(rows, None), P("prompt", None),
        ),
        out_specs=(whole, whole, P(None, None, "fsdp")),
        check_vma=False,
    )
```

time: 85.6 us -> 66.8 us (0.78)
  the two profiles are of different devices: /device:TPU:6 before, /device:TPU:1 now
where the time goes in v2:
time: 66.8 us; the launch traced here: 66.4 us
  Pallas kernels  62.6 us (94%)
  local copies, waits for them, and re-layouts  3.12 us (5%)
    pallas_call x1, Pallas kernels, on_device(): pl.pallas_call(functools.partial(kernel, scale), out_shape=(jax.ShapeDtyp...  62.6 us
    unnamed x7, local copies, waits for them, and re-layouts  3.12 us

profile of v2, /device:TPU:1, one launch (start us, length us, event | category | flops | bytes accessed | tf_op | source)
XLA Modules:
  0.0 66.4 jit_solution(7056225492038265736)
XLA Ops:
  0.6 62.6 %adapter_backward.1 = (f32[1,128,128]{2,1,0:T(8,128)}, f32[1,256,128]{2,1,0:T(8,128)}, f32[2,64,256]{2,1,0:T(8,128)}) custom-call(bf16[1,128,2048]{2,1,0:T(8,128)(2,1)} %pq_h.1, bf16[1,128,256]{2,1,0:T(8,128)(2,1)} %pk_h.1, bf16[1,128,256]{2,1,0:T(8,128)(2,1)} %pv_h.1, bf16[1,128,128]{2,1,0:T(8,128)(2,1)} %pa_h.1, bf16[1,128,2048]{2,1,0:T(8,128)(2,1)} %pg_h.1, ...), custom_call_target="tpu_custom_call" | custom-call | tf_op jit(solution)/shard_map/adapter_backward/pallas_call | solution.py:356
  63.2 0.0 copy-start.1
  63.2 1.5 %copy.19 = f32[1,128,128]{2,1,0:T(8,128)} copy(f32[1,128,128]{2,1,0:T(8,128)} %get-tuple-element.6) | data formatting | bytes 131072
  64.7 0.0 copy-done.1
  64.7 0.0 copy-start
  64.7 0.7 copy.20
  65.4 0.3 copy-done
  65.7 0.7 copy.21
Async XLA Ops:
  63.2 1.5 %copy-start.1 = (f32[1,256,128]{2,1,0:T(8,128)S(1)}, f32[1,256,128]{2,1,0:T(8,128)}, u32[]{:S(2)}) copy-start(f32[1,256,128]{2,1,0:T(8,128)} %get-tuple-element.7) | copy-start | bytes 393220
  64.7 1.0 %copy-start = (f32[2,64,256]{2,1,0:T(8,128)S(1)}, f32[2,64,256]{2,1,0:T(8,128)}, u32[]{:S(2)}) copy-start(f32[2,64,256]{2,1,0:T(8,128)} %get-tuple-element.8) | copy-start | bytes 393220

commit v3 on v2

--- a/solution.py
+++ b/solution.py
@@ -50,12 +50,32 @@
     return probs.astype(jnp.bfloat16), dscores.astype(jnp.bfloat16)
 
 
+def joined_tile(keys, values, queries, grads, own_weights, own_dprobs, own_stats, live):
+    scores = mm(keys, queries, NT)
+    dprobs = mm(values, grads, NT)
+    own_highest, own_sum, own_dot = own_stats[0:1], own_stats[1:2], own_stats[2:3]
+    highest = jnp.maximum(own_highest, jnp.max(scores, axis=0, keepdims=True))
+    weights = jnp.exp2((scores - highest) * EXP2_FACTOR)
+    rescale = jnp.exp2((own_highest - highest) * EXP2_FACTOR)
+    total = own_sum * rescale + jnp.sum(weights, axis=0, keepdims=True)
+    inverse = jnp.where(live, 1.0 / total, 0.0)
+    delta = (own_dot * rescale + jnp.sum(weights * dprobs, axis=0, keepdims=True)) * inverse
+    probs = weights * inverse
+    own_probs = own_weights * (rescale * inverse)
+    return (
+        probs.astype(jnp.bfloat16),
+        (probs * (dprobs - delta)).astype(jnp.bfloat16),
+        own_probs.astype(jnp.bfloat16),
+        (own_probs * (own_dprobs - delta)).astype(jnp.bfloat16),
+    )
+
+
 def kernel(
     scale,
     pq_h, pk_h, pv_h, pa_h, pg_h, aq_h, ak_h, av_h, aa_h, ag_h, up_h, lens_h, pairing_h,
     prompt_out, answer_out, up_out,
     pq, pk, pv, pa, pg, aq, ak, av, aa, ag, up, lens, pairing,
-    wide_up, kv_own, kv_slot, kv_pre, mid1, mid2, amid1, amid2, a_pre,
+    wide_up, kv_own, kv_slot, kv_pre, mid1, mid2, amid1, amid2, a_pre, a_cols, own_w, own_dp, own_st,
     probs_s, dsc_s, dkv, own_proj, outer_acc,
     own_half, own_twin, pre_part, pre_twin, pre_half, pre_x, pre_z, pre_pick, pre_home, done_half, done_twin,
     an_send, an_recv, gr_send, gr1, gr2_send, gr2, gr3_send, gr3,
@@ -197,38 +217,60 @@
     kv_slot[:, 0:256] = (ak[...].astype(jnp.float32) + lifted_slots[:, 0:256]).astype(jnp.bfloat16)
     kv_slot[:, 256:512] = (av[...].astype(jnp.float32) + lifted_slots[:, 256:512]).astype(jnp.bfloat16)
     outer_acc[...] = mm(pa[...], dkv[0:128, :], TN)
-
-    ready(kv_pre.at[pl.ds(0, 240)], recv_sem.at[2])
+    a_cols[:, 128:256] = jnp.transpose(aa[0:128, :])
+    a_cols[:, 256:384] = jnp.transpose(aa[128:256, :])
+
     row_at = lax.rem(lax.broadcasted_iota(jnp.int32, (1, 256), 1), T)
 
-    def slot_head(h, carry):
-        at = pl.multiple_of(h * HD, HD)
-        value_at = pl.multiple_of(256 + h * HD, HD)
+    def heads(ref, c, h, g, count):
+        return jnp.concatenate(
+            [ref[c * T:(c + 1) * T, (8 * h + g + i) * HD:(8 * h + g + i + 1) * HD] for i in range(count)], axis=0
+        )
+
+    for h in range(2):
+        for c in range(2):
+            keys = kv_slot[c * T:(c + 1) * T, h * HD:(h + 1) * HD]
+            values = kv_slot[c * T:(c + 1) * T, 256 + h * HD:256 + (h + 1) * HD]
+            for g in range(0, 8, 2):
+                cols = slice(g * HD, (g + 2) * HD)
+                scores = jnp.where(visible, mm(keys, heads(aq, c, h, g, 2), NT), -1e30)
+                dprobs = mm(values, heads(ag, c, h, g, 2), NT)
+                highest = jnp.max(scores, axis=0, keepdims=True)
+                weights = jnp.exp2((scores - highest) * EXP2_FACTOR)
+                own_w[2 * h + c, :, cols] = weights
+                own_dp[2 * h + c, :, cols] = dprobs
+                own_st[2 * h + c, 0:1, cols] = highest
+                own_st[2 * h + c, 1:2, cols] = jnp.sum(weights, axis=0, keepdims=True)
+                own_st[2 * h + c, 2:3, cols] = jnp.sum(weights * dprobs, axis=0, keepdims=True)
+
+    def slot_head(h):
+        key_cols = slice(h * HD, (h + 1) * HD)
+        value_cols = slice(256 + h * HD, 256 + (h + 1) * HD)
+        keys, values = kv_pre[0:128, key_cols], kv_pre[128:256, key_cols]
         key_sum, value_sum = 0.0, 0.0
         for c in range(2):
-            part = slice(c * T, (c + 1) * T)
-            keys = jnp.concatenate([kv_pre[0:128, pl.ds(at, HD)], kv_slot[part, pl.ds(at, HD)]], axis=0)
-            values = jnp.concatenate([kv_pre[128:256, pl.ds(at, HD)], kv_slot[part, pl.ds(value_at, HD)]], axis=0)
             live = row_at < lens[0, c]
-
-            def heads(ref, g, count):
-                return jnp.concatenate(
-                    [ref[part, pl.ds(pl.multiple_of(h * 1024 + (g + i) * HD, HD), HD)] for i in range(count)], axis=0
+            for g in range(0, 8, 2):
+                cols = slice(g * HD, (g + 2) * HD)
+                probs, dscores, own_probs, own_dscores = joined_tile(
+                    keys, values, heads(aq, c, h, g, 2), heads(ag, c, h, g, 2),
+                    own_w[2 * h + c, :, cols], own_dp[2 * h + c, :, cols], own_st[2 * h + c, :, cols], live,
                 )
-
-            for g in range(0, 8, 2):
-                probs, dscores = backward_tile(keys, values, heads(aq, g, 2), heads(ag, g, 2), visible, live, T)
-                probs_s[c, :, g * HD:(g + 2) * HD] = probs
-                dsc_s[c, :, g * HD:(g + 2) * HD] = dscores
-            key_grad = mm(dsc_s[c], heads(aq, 0, 8), NN) * FACTOR
-            value_grad = mm(probs_s[c], heads(ag, 0, 8), NN)
-            dkv[256 + c * T:256 + (c + 1) * T, pl.ds(at, HD)] = key_grad[T:].astype(jnp.bfloat16)
-            dkv[256 + c * T:256 + (c + 1) * T, pl.ds(value_at, HD)] = value_grad[T:].astype(jnp.bfloat16)
+                probs_s[c, 0:128, cols] = probs
+                probs_s[c, 128:256, cols] = own_probs
+                dsc_s[c, 0:128, cols] = dscores
+                dsc_s[c, 128:256, cols] = own_dscores
+            key_grad = mm(dsc_s[c], heads(aq, c, h, 0, 8), NN) * FACTOR
+            value_grad = mm(probs_s[c], heads(ag, c, h, 0, 8), NN)
+            dkv[256 + c * T:256 + (c + 1) * T, key_cols] = key_grad[T:].astype(jnp.bfloat16)
+            dkv[256 + c * T:256 + (c + 1) * T, value_cols] = value_grad[T:].astype(jnp.bfloat16)
             key_sum = key_sum + key_grad[:T]
             value_sum = value_sum + value_grad[:T]
-        dkv[128:256, pl.ds(at, HD)] = key_sum.astype(jnp.bfloat16)
-        dkv[128:256, pl.ds(value_at, HD)] = value_sum.astype(jnp.bfloat16)
-        return carry
+        dkv[128:256, key_cols] = key_sum.astype(jnp.bfloat16)
+        dkv[128:256, value_cols] = value_sum.astype(jnp.bfloat16)
+
+    ready(kv_pre.at[pl.ds(0, 240)], recv_sem.at[2])
+    slot_head(0)
 
     @pl.when(is_mid)
     def _():
@@ -240,22 +282,24 @@
 
     a_copy = to(a_pre.at[rows(f, 64)], a_pre.at[rows(f, 64)], 5, twin)
     a_copy.start()
-
-    lax.fori_loop(0, 2, slot_head, 0)
+    slot_head(1)
+
+    ready(a_pre.at[pl.ds(0, 64)], recv_sem.at[5])
+    a_cols[:, 0:128] = jnp.transpose(a_pre[...])
+    for b, (row, col) in enumerate([(0, 0), (0, 128), (64, 256), (64, 384)]):
+        block = outer_acc[row:row + 64, col:col + 128] + mm(
+            a_cols[row:row + 64, :], dkv[128:512, col:col + 128], NN
+        )
+        gr_send[4 * b:4 * b + 4] = block.astype(jnp.bfloat16).reshape(4, 16, 128)
+    for k in PLANE_ORDER:
+        peer = (lax.rem(y + k // 4, 4)) * 4 + lax.rem(x + k % 4, 4)
+        to(gr_send.at[peer], gr1.at[plane], 7, in_plane(peer)).start()
+    gr1[plane] = gr_send[plane]
 
     pre_part[...] = mm(dkv[128:256, :], wide_up[...], NT)
     pre_half[0] = pre_part[rows(1 - f, 64), :].astype(jnp.bfloat16)
     pre_copy = to(pre_half.at[0], pre_twin, 6, twin)
     pre_copy.start()
-
-    ready(a_pre.at[pl.ds(0, 64)], recv_sem.at[5])
-    outer = outer_acc[...] + mm(a_pre[...], dkv[128:256, :], TN) + mm(aa[...], dkv[256:512, :], TN)
-    for b, (row, col) in enumerate([(0, 0), (0, 128), (64, 256), (64, 384)]):
-        gr_send[4 * b:4 * b + 4] = outer[row:row + 64, col:col + 128].astype(jnp.bfloat16).reshape(4, 16, 128)
-    for k in PLANE_ORDER:
-        peer = (lax.rem(y + k // 4, 4)) * 4 + lax.rem(x + k % 4, 4)
-        to(gr_send.at[peer], gr1.at[plane], 7, in_plane(peer)).start()
-    gr1[plane] = gr_send[plane]
 
     ready(pre_twin, recv_sem.at[6])
     pre_half[1] = (pre_part[rows(f, 64), :] + pre_twin[...].astype(jnp.float32)).astype(jnp.bfloat16)
@@ -348,12 +392,21 @@
         ready(amid1.at[pl.ds(0, 4)], send_sem.at[1])
 
 
+def store(a, b, c, a_out, b_out, c_out, sem):
+    copies = [pltpu.make_async_copy(*pair, sem.at[i]) for i, pair in enumerate([(a, a_out), (b, b_out), (c, c_out)])]
+    for copy in copies:
+        copy.start()
+    for copy in copies:
+        copy.wait()
+
+
 def on_device(scale, *args):
     bf, f32 = jnp.bfloat16, jnp.float32
     hbm = pl.BlockSpec(memory_space=pltpu.HBM)
     vmem = pl.BlockSpec(memory_space=pltpu.VMEM)
     V = pltpu.VMEM
-    return pl.pallas_call(
+    args = [pltpu.with_memory_space_constraint(a, pltpu.HBM) for a in args]
+    held = pl.pallas_call(
         functools.partial(kernel, scale),
         out_shape=(
             jax.ShapeDtypeStruct((1, 128, 128), f32),
@@ -368,6 +421,7 @@
             V((2, 64, 256), bf), pltpu.SMEM((1, 2), jnp.int32), pltpu.SMEM((1, 16), jnp.int32),
             V((128, 512), bf), V((256, 256), bf), V((256, 512), bf), V((256, 256), bf),
             V((16, 16, 256), bf), V((16, 16, 256), bf), V((16, 16, 128), bf), V((16, 16, 128), bf), V((128, 128), bf),
+            V((128, 384), bf), V((4, 128, 1024), f32), V((4, 128, 1024), f32), V((4, 8, 1024), f32),
             V((2, 256, 1024), bf), V((2, 256, 1024), bf), V((512, 512), bf), V((128, 128), f32), V((128, 512), f32),
             V((64, 128), bf), V((64, 128), bf), V((128, 128), f32), V((64, 128), bf), V((2, 64, 128), bf),
             V((4, 16, 128), bf), V((4, 4, 16, 128), bf), V((4, 16, 128), bf), V((4, 16, 128), bf),
@@ -378,10 +432,19 @@
             pltpu.SemaphoreType.DMA((13,)), pltpu.SemaphoreType.DMA((15,)), pltpu.SemaphoreType.DMA((15,)),
         ],
         compiler_params=pltpu.CompilerParams(
-            collective_id=0, has_side_effects=True, vmem_limit_bytes=60 * 1024 * 1024
+            collective_id=0, has_side_effects=True, vmem_limit_bytes=48 * 1024 * 1024
         ),
         name="adapter_backward",
     )(*args)
+    return pl.pallas_call(
+        store,
+        out_shape=tuple(jax.ShapeDtypeStruct(h.shape, h.dtype) for h in held),
+        in_specs=[pl.BlockSpec(memory_space=pl.ANY)] * 3,
+        out_specs=(pl.BlockSpec(memory_space=pl.ANY),) * 3,
+        scratch_shapes=[pltpu.SemaphoreType.DMA((3,))],
+        compiler_params=pltpu.CompilerParams(vmem_limit_bytes=65136 * 1024),
+        name="store",
+    )(*[pltpu.with_memory_space_constraint(h, pltpu.VMEM) for h in held])
 
 
 def solution(mesh):

time: 66.8 us -> 62.2 us (0.931)
  local copies, waits for them, and re-layouts: 3.12 us -> 0 us
  Pallas kernels: 62.6 us -> 61.4 us
    unnamed x7 -> x0, local copies, waits for them, and re-layouts: 3.12 us -> none
    pallas_call x1, Pallas kernels: 62.6 us -> 60.6 us  [on_device(): pl.pallas_call(functools.partial(kernel, scale), out_shape=(jax.ShapeDtyp...]
    pallas_call x0 -> x1, Pallas kernels: none -> 0.75 us  [on_device(): pl.pallas_call(store, out_shape=tuple((jax.ShapeDtypeStruct(h.shape, h.dt...]
where the time goes in v3:
time: 62.2 us; the launch traced here: 62 us
  Pallas kernels  61.4 us (99%)
  between operations  0.64 us (1%)
    pallas_call x1, Pallas kernels, on_device(): pl.pallas_call(functools.partial(kernel, scale), out_shape=(jax.ShapeDtyp...  60.6 us

profile of v3, /device:TPU:1, one launch (start us, length us, event | category | flops | bytes accessed | tf_op | source)
XLA Modules:
  0.0 62.0 jit_solution(16835166570721349897)
XLA Ops:
  0.6 60.6 %adapter_backward.1 = (f32[1,128,128]{2,1,0:T(8,128)S(1)}, f32[1,256,128]{2,1,0:T(8,128)S(1)}, f32[2,64,256]{2,1,0:T(8,128)S(1)}) custom-call(bf16[1,128,2048]{2,1,0:T(8,128)(2,1)} %pq_h.1, bf16[1,128,256]{2,1,0:T(8,128)(2,1)} %pk_h.1, bf16[1,128,256]{2,1,0:T(8,128)(2,1)} %pv_h.1, bf16[1,128,128]{2,1,0:T(8,128)(2,1)} %pa_h.1, bf16[1,128,2048]{2,1,0:T(8,128)(2,1)} %pg_h.1, ...), custom_call_target="tpu_custom_call" | custom-call | tf_op jit(solution)/shard_map/adapter_backward/pallas_call | solution.py:409
  61.3 0.7 %store.1 = (f32[1,128,128]{2,1,0:T(8,128)}, f32[1,256,128]{2,1,0:T(8,128)}, f32[2,64,256]{2,1,0:T(8,128)}) custom-call(f32[1,128,128]{2,1,0:T(8,128)S(1)} %get-tuple-element.6.a, f32[1,256,128]{2,1,0:T(8,128)S(1)} %get-tuple-element.7.b, f32[2,64,256]{2,1,0:T(8,128)S(1)} %get-tuple-element.8.c), custom_call_target="tpu_custom_call" | custom-call | tf_op jit(solution)/shard_map/store/pallas_call | solution.py:439

commit v4 on v3

--- a/solution.py
+++ b/solution.py
@@ -17,6 +17,8 @@
 NN = (((1,), (0,)), ((), ()))
 FACTOR = 1.0 / math.sqrt(HD)
 EXP2_FACTOR = FACTOR * math.log2(math.e)
+SHIFTS = (0, 1, 3)
+NEAR_ORDER = ((1, 2), (2, 2), (1, 1), (2, 1), (1, 3), (2, 3), (1, 0), (2, 0), (0, 2), (0, 1), (0, 3))
 RESP_ORDER = (10, 9, 11, 8, 6, 14, 5, 7, 13, 15, 4, 12, 2, 1, 3)
 PLANE_ORDER = (10, 9, 11, 6, 14, 8, 2, 5, 7, 13, 15, 4, 12, 1, 3)
 RING_ORDER = (8, 7, 9, 6, 10, 5, 11, 4, 12, 3, 13, 2, 14, 1, 15)
@@ -75,7 +77,7 @@
     pq_h, pk_h, pv_h, pa_h, pg_h, aq_h, ak_h, av_h, aa_h, ag_h, up_h, lens_h, pairing_h,
     prompt_out, answer_out, up_out,
     pq, pk, pv, pa, pg, aq, ak, av, aa, ag, up, lens, pairing,
-    wide_up, kv_own, kv_slot, kv_pre, mid1, mid2, amid1, amid2, a_pre, a_cols, own_w, own_dp, own_st,
+    wide_up, pack, kv_slot, pre, mid1, mid2, got, a_pre, a_cols, own_w, own_dp, own_st,
     probs_s, dsc_s, dkv, own_proj, outer_acc,
     own_half, own_twin, pre_part, pre_twin, pre_half, pre_x, pre_z, pre_pick, pre_home, done_half, done_twin,
     an_send, an_recv, gr_send, gr1, gr2_send, gr2, gr3_send, gr3,
@@ -87,7 +89,6 @@
     twin = {"fsdp": 1 - f}
     x, z_hi = lax.rem(r, 4), r // 4
     y, z_lo = p // 4, lax.rem(p, 4)
-    is_mid = lax.rem(r, 4) == 2 * f
     plane = y * 4 + x
     ring = z_hi * 4 + z_lo
 
@@ -108,8 +109,8 @@
     def greet(where):
         pl.semaphore_signal(barrier, inc=1, device_id=where, device_id_type=MESH)
 
-    for k in RESP_ORDER:
-        greet({"resp": lax.rem(r + k, N)})
+    for shift, k in NEAR_ORDER:
+        greet({"resp": lax.rem(z_hi + SHIFTS[shift], 4) * 4 + lax.rem(x + k, 4)})
 
     loads = [
         pltpu.make_async_copy(src.at[0] if lead else src, dst, load_sem.at[i])
@@ -125,8 +126,8 @@
     greet(twin)
     for k in range(4, N):
         greet({"prompt": (lax.rem(y + k // 4, 4)) * 4 + z_lo, "resp": along_x(k % 4)})
-    for k in range(4, N):
-        greet({"prompt": y * 4 + lax.rem(z_lo + k // 4, 4), "resp": along_z(k % 4)})
+    for k in range(1, 4):
+        greet({"prompt": y * 4 + lax.rem(z_lo + k, 4)})
 
     wide_up[...] = jnp.zeros_like(wide_up)
     for load in loads[:4]:
@@ -134,10 +135,13 @@
     wide_up[0:64, 0:256] = up[0]
     wide_up[64:128, 256:512] = up[1]
     lifted = mm(pa[...], wide_up[...], NN)
-    kv_own[0:128, :] = (pk[...].astype(jnp.float32) + lifted[:, 0:256]).astype(jnp.bfloat16)
-    kv_own[128:256, :] = (pv[...].astype(jnp.float32) + lifted[:, 256:512]).astype(jnp.bfloat16)
-
-    pl.semaphore_wait(barrier, 40)
+    for i, base in enumerate((pk, pv)):
+        full = (base[...].astype(jnp.float32) + lifted[:, 256 * i:256 * i + 256]).astype(jnp.bfloat16)
+        for h in range(2):
+            pack[16 * i + 8 * h:16 * i + 8 * h + 8] = full[:, h * HD:(h + 1) * HD].reshape(8, 16, HD)
+    pack[32:36] = pa[pl.ds(pl.multiple_of(f * 64, 64), 64), :].reshape(4, 16, HD)
+
+    pl.semaphore_wait(barrier, 27)
 
     def to(src, dst, lane, where):
         return pltpu.make_async_remote_copy(
@@ -148,20 +152,13 @@
     def rows(index, size=16):
         return pl.ds(pl.multiple_of(index * size, size), size)
 
-    for k in RESP_ORDER:
-        peer = lax.rem(r + k, N)
-        to(kv_own.at[rows(peer)], mid1.at[r], 0, {"resp": peer}).start()
-    mid1[r] = kv_own[rows(r), :]
-    for i in range(4):
-        member = 4 * i + 2 * f
-
-        @pl.when(member != r)
-        def _():
-            to(pa.at[rows(4 * f + i)], amid1.at[r], 1, {"resp": member}).start()
-
-    @pl.when(is_mid)
-    def _():
-        amid1[r] = pa[rows(4 * f + z_hi), :]
+    for shift, k in NEAR_ORDER:
+        peer_x = lax.rem(x + k, 4)
+        peer = lax.rem(z_hi + SHIFTS[shift], 4) * 4 + peer_x
+        to(pack.at[pl.ds(3 * (4 * shift + peer_x), 3)], mid1.at[r], 0, {"resp": peer}).start()
+    mid1[r] = pack[pl.ds(3 * x, 3)]
+    for k in range(4):
+        mid1[lax.rem(z_hi + 2, 4) * 4 + k] = jnp.zeros((3, 16, HD), jnp.bfloat16)
 
     lane_at = lax.rem(lax.broadcasted_iota(jnp.int32, (T, 256), 1), T)
     visible = lax.broadcasted_iota(jnp.int32, (T, 256), 0) <= lane_at
@@ -170,8 +167,8 @@
 
     def own_head(h, carry):
         at = pl.multiple_of(h * HD, HD)
-        keys = kv_own[0:128, pl.ds(at, HD)]
-        values = kv_own[128:256, pl.ds(at, HD)]
+        keys = pack[pl.ds(8 * h, 8)].reshape(T, HD)
+        values = pack[pl.ds(16 + 8 * h, 8)].reshape(T, HD)
 
         def heads(ref, g, count):
             return jnp.concatenate(
@@ -191,21 +188,17 @@
     lax.fori_loop(0, 2, own_head, 0)
 
     loads[12].wait()
-    ready(mid1.at[pl.ds(0, 15)], recv_sem.at[0])
+    ready(mid1.at[pl.ds(0, 11)], recv_sem.at[0])
+
+    def held_of(member):
+        owner = pairing[0, member]
+        return jnp.where(lax.rem(owner // 4 + 6 - z_hi, 4) == 0, r, owner)
+
     for k in RESP_ORDER:
         peer = lax.rem(r + k, N)
-        mid2[peer] = mid1[pairing[0, peer]]
-        to(mid2.at[peer], kv_pre.at[rows(r)], 2, {"resp": peer}).start()
-    kv_pre[rows(r), :] = mid1[pairing[0, r]]
-
-    @pl.when(is_mid)
-    def _():
-        ready(amid1.at[pl.ds(0, 15)], recv_sem.at[1])
-        for k in RESP_ORDER:
-            peer = lax.rem(r + k, N)
-            amid2[peer] = amid1[pairing[0, peer]]
-            to(amid2.at[peer], a_pre.at[rows(4 * f + z_hi)], 3, {"resp": peer}).start()
-        a_pre[rows(4 * f + z_hi), :] = amid1[pairing[0, r]]
+        mid2[peer] = mid1[held_of(peer)]
+        to(mid2.at[peer], got.at[r], 2, {"resp": peer}).start()
+    got[r] = mid1[held_of(r)]
 
     own_proj[...] = mm(dkv[0:128, :], wide_up[...], NT)
     own_half[...] = own_proj[rows(1 - f, 64), :].astype(jnp.bfloat16)
@@ -246,7 +239,8 @@
     def slot_head(h):
         key_cols = slice(h * HD, (h + 1) * HD)
         value_cols = slice(256 + h * HD, 256 + (h + 1) * HD)
-        keys, values = kv_pre[0:128, key_cols], kv_pre[128:256, key_cols]
+        keys = pre[8 * h:8 * h + 8].reshape(T, HD)
+        values = pre[16 + 8 * h:24 + 8 * h].reshape(T, HD)
         key_sum, value_sum = 0.0, 0.0
         for c in range(2):
             live = row_at < lens[0, c]
@@ -269,19 +263,17 @@
         dkv[128:256, key_cols] = key_sum.astype(jnp.bfloat16)
         dkv[128:256, value_cols] = value_sum.astype(jnp.bfloat16)
 
-    ready(kv_pre.at[pl.ds(0, 240)], recv_sem.at[2])
-    slot_head(0)
-
-    @pl.when(is_mid)
-    def _():
-        ready(a_pre.at[pl.ds(0, 48)], recv_sem.at[3])
-
-    @pl.when(jnp.logical_not(is_mid))
-    def _():
-        ready(a_pre.at[pl.ds(0, 64)], recv_sem.at[3])
-
+    ready(got.at[pl.ds(0, 15)], recv_sem.at[2])
+    from_plane = pairing[0, r] // 4
+    for shift in range(3):
+        for k in range(4):
+            at = 3 * (4 * shift + k)
+            pre[at:at + 3] = got[lax.rem(from_plane + SHIFTS[shift], 4) * 4 + k]
+
+    a_pre[rows(f, 64), :] = pre[32:36].reshape(64, HD)
     a_copy = to(a_pre.at[rows(f, 64)], a_pre.at[rows(f, 64)], 5, twin)
     a_copy.start()
+    slot_head(0)
     slot_head(1)
 
     ready(a_pre.at[pl.ds(0, 64)], recv_sem.at[5])
@@ -368,7 +360,7 @@
             gr3[4 * b:4 * b + 4].reshape(64, 128).astype(jnp.float32)
         )
 
-    ready(mid1.at[pl.ds(0, 15)], send_sem.at[0])
+    ready(mid1.at[pl.ds(0, 11)], send_sem.at[0])
     ready(mid2.at[pl.ds(0, 15)], send_sem.at[2])
     own_copy.wait_send()
     a_copy.wait_send()
@@ -381,15 +373,6 @@
     ready(pre_pick.at[pl.ds(0, 3)], send_sem.at[12])
     ready(gr3.at[pl.ds(0, 15)], send_sem.at[13])
     done_copy.wait_send()
-
-    @pl.when(is_mid)
-    def _():
-        ready(amid1.at[pl.ds(0, 3)], send_sem.at[1])
-        ready(amid2.at[pl.ds(0, 15)], send_sem.at[3])
-
-    @pl.when(jnp.logical_not(is_mid))
-    def _():
-        ready(amid1.at[pl.ds(0, 4)], send_sem.at[1])
 
 
 def store(a, b, c, a_out, b_out, c_out, sem):
@@ -419,8 +402,8 @@
             V((128, 2048), bf), V((128, 256), bf), V((128, 256), bf), V((128, 128), bf), V((128, 2048), bf),
             V((256, 2048), bf), V((256, 256), bf), V((256, 256), bf), V((256, 128), bf), V((256, 2048), bf),
             V((2, 64, 256), bf), pltpu.SMEM((1, 2), jnp.int32), pltpu.SMEM((1, 16), jnp.int32),
-            V((128, 512), bf), V((256, 256), bf), V((256, 512), bf), V((256, 256), bf),
-            V((16, 16, 256), bf), V((16, 16, 256), bf), V((16, 16, 128), bf), V((16, 16, 128), bf), V((128, 128), bf),
+            V((128, 512), bf), V((36, 16, 128), bf), V((256, 512), bf), V((36, 16, 128), bf),
+            V((16, 3, 16, 128), bf), V((16, 3, 16, 128), bf), V((16, 3, 16, 128), bf), V((128, 128), bf),
             V((128, 384), bf), V((4, 128, 1024), f32), V((4, 128, 1024), f32), V((4, 8, 1024), f32),
             V((2, 256, 1024), bf), V((2, 256, 1024), bf), V((512, 512), bf), V((128, 128), f32), V((128, 512), f32),
             V((64, 128), bf), V((64, 128), bf), V((128, 128), f32), V((64, 128), bf), V((2, 64, 128), bf),

time: 62.2 us -> 58.6 us (0.942); the launches traced: 62 us -> 57.7 us
  Pallas kernels: 61.4 us -> 57.1 us
    pallas_call x1, Pallas kernels: 60.6 us -> 56.3 us  [on_device(): pl.pallas_call(functools.partial(kernel, scale), out_shape=(jax.ShapeDtyp...]
where the time goes in v4:
time: 58.6 us; the launch traced here: 57.7 us
  Pallas kernels  57.1 us (97%)
  between operations  0.64 us (1%)
    pallas_call x1, Pallas kernels, on_device(): pl.pallas_call(functools.partial(kernel, scale), out_shape=(jax.ShapeDtyp...  56.3 us

profile of v4, /device:TPU:1, one launch (start us, length us, event | category | flops | bytes accessed | tf_op | source)
XLA Modules:
  0.0 57.7 jit_solution(4005365183471167217)
XLA Ops:
  0.6 56.3 %adapter_backward.1 = (f32[1,128,128]{2,1,0:T(8,128)S(1)}, f32[1,256,128]{2,1,0:T(8,128)S(1)}, f32[2,64,256]{2,1,0:T(8,128)S(1)}) custom-call(bf16[1,128,2048]{2,1,0:T(8,128)(2,1)} %pq_h.1, bf16[1,128,256]{2,1,0:T(8,128)(2,1)} %pk_h.1, bf16[1,128,256]{2,1,0:T(8,128)(2,1)} %pv_h.1, bf16[1,128,128]{2,1,0:T(8,128)(2,1)} %pa_h.1, bf16[1,128,2048]{2,1,0:T(8,128)(2,1)} %pg_h.1, ...), custom_call_target="tpu_custom_call" | custom-call | tf_op jit(solution)/shard_map/adapter_backward/pallas_call | solution.py:392
  56.9 0.7 %store.1 = (f32[1,128,128]{2,1,0:T(8,128)}, f32[1,256,128]{2,1,0:T(8,128)}, f32[2,64,256]{2,1,0:T(8,128)}) custom-call(f32[1,128,128]{2,1,0:T(8,128)S(1)} %get-tuple-element.6.a, f32[1,256,128]{2,1,0:T(8,128)S(1)} %get-tuple-element.7.b, f32[2,64,256]{2,1,0:T(8,128)S(1)} %get-tuple-element.8.c), custom_call_target="tpu_custom_call" | custom-call | tf_op jit(solution)/shard_map/store/pallas_call | solution.py:422

commit v5 on v4

--- a/solution.py
+++ b/solution.py
@@ -79,7 +79,7 @@
     pq, pk, pv, pa, pg, aq, ak, av, aa, ag, up, lens, pairing,
     wide_up, pack, kv_slot, pre, mid1, mid2, got, a_pre, a_cols, own_w, own_dp, own_st,
     probs_s, dsc_s, dkv, own_proj, outer_acc,
-    own_half, own_twin, pre_part, pre_twin, pre_half, pre_x, pre_z, pre_pick, pre_home, done_half, done_twin,
+    own_half, own_twin, pre_part, pre_twin, pre_half, pre_z, pre_pick, pre_home, done_half, done_twin,
     an_send, an_recv, gr_send, gr1, gr2_send, gr2, gr3_send, gr3,
     load_sem, send_sem, recv_sem,
 ):
@@ -293,21 +293,16 @@
     pre_copy = to(pre_half.at[0], pre_twin, 6, twin)
     pre_copy.start()
 
-    ready(pre_twin, recv_sem.at[6])
-    pre_half[1] = (pre_part[rows(f, 64), :] + pre_twin[...].astype(jnp.float32)).astype(jnp.bfloat16)
-    for k in (2, 1, 3):
-        peer_x = lax.rem(x + k, 4)
-        to(pre_half.at[1, rows(peer_x)], pre_x.at[x], 8, {"resp": z_hi * 4 + peer_x}).start()
-    pre_x[x] = pre_half[1, rows(x), :]
-
     an_send[...] = mm(dkv[256:512, :], wide_up[...], NT).astype(jnp.bfloat16)
     to_twin = to(an_send, an_recv, 9, twin)
+
+    ready(pre_twin, recv_sem.at[6])
+    both = (pre_part[rows(f, 64), :] + pre_twin[...].astype(jnp.float32)).astype(jnp.bfloat16)
+    pre_half[1] = both
+    for k in (2, 1, 3):
+        to(pre_half.at[1], pre_z.at[z_hi], 10, {"resp": along_z(k)}).start()
+    pre_z[z_hi] = both
     to_twin.start()
-
-    ready(pre_x.at[pl.ds(0, 3)], recv_sem.at[8])
-    for k in (2, 1, 3):
-        to(pre_x, pre_z.at[z_hi], 10, {"resp": along_z(k)}).start()
-    pre_z[z_hi] = pre_x[...]
 
     ready(gr1.at[pl.ds(0, 15)], recv_sem.at[7])
     part_sum = jnp.sum(gr1[...].astype(jnp.float32), axis=0).astype(jnp.bfloat16)
@@ -328,10 +323,13 @@
     sources = [responder(along_x(k)) for k in range(4)]
     ready(own_twin, recv_sem.at[4])
     ready(pre_z.at[pl.ds(0, 3)], recv_sem.at[10])
-    for k in (2, 1, 3):
-        pre_pick[k] = pre_z[sources[k] // 4, lax.rem(sources[k], 4)]
-        to(pre_pick.at[k], pre_home.at[x], 12, {"resp": along_x(k)}).start()
-    pre_home[x] = pre_z[sources[0] // 4, lax.rem(sources[0], 4)]
+    for k in (2, 1, 3, 0):
+        mine = pre_z[jnp.where(lax.rem(sources[k], 4) == x, sources[k] // 4, z_hi)]
+        if k:
+            pre_pick[k] = mine
+            to(pre_pick.at[k], pre_home.at[x], 12, {"resp": along_x(k)}).start()
+        else:
+            pre_home[x] = mine
 
     ready(gr2.at[pl.ds(0, 15)], recv_sem.at[11])
     total = (jnp.sum(gr2[...].astype(jnp.float32), axis=0) * scale).astype(jnp.bfloat16)
@@ -345,7 +343,7 @@
     done = (
         own_proj[rows(f, 64), :]
         + own_twin[...].astype(jnp.float32)
-        + pre_home[...].reshape(64, 128).astype(jnp.float32)
+        + pre_home[lax.rem(sources[0], 4)].astype(jnp.float32)
     )
     done_half[...] = done
     done_copy = to(done_half, done_twin, 14, twin)
@@ -366,7 +364,6 @@
     a_copy.wait_send()
     pre_copy.wait_send()
     ready(gr_send.at[pl.ds(0, 15)], send_sem.at[7])
-    ready(pre_x.at[pl.ds(0, 3)], send_sem.at[8])
     to_twin.wait_send()
     ready(pre_z.at[pl.ds(0, 3)], send_sem.at[10])
     ready(gr2.at[pl.ds(0, 15)], send_sem.at[11])
@@ -407,7 +404,7 @@
             V((128, 384), bf), V((4, 128, 1024), f32), V((4, 128, 1024), f32), V((4, 8, 1024), f32),
             V((2, 256, 1024), bf), V((2, 256, 1024), bf), V((512, 512), bf), V((128, 128), f32), V((128, 512), f32),
             V((64, 128), bf), V((64, 128), bf), V((128, 128), f32), V((64, 128), bf), V((2, 64, 128), bf),
-            V((4, 16, 128), bf), V((4, 4, 16, 128), bf), V((4, 16, 128), bf), V((4, 16, 128), bf),
+            V((4, 64, 128), bf), V((4, 64, 128), bf), V((4, 64, 128), bf),
             V((64, 128), f32), V((64, 128), f32),
             V((256, 128), bf), V((256, 128), bf),
             V((16, 16, 128), bf), V((16, 16, 128), bf), V((16, 128), bf), V((16, 16, 128), bf),

time: 58.6 us -> 55.6 us (0.949)
  the two profiles are of different devices: /device:TPU:1 before, /device:TPU:32 now
where the time goes in v5:
time: 55.6 us; the launch traced here: 55.5 us
  Pallas kernels  54.9 us (99%)
  between operations  0.64 us (1%)
    pallas_call x1, Pallas kernels, on_device(): pl.pallas_call(functools.partial(kernel, scale), out_shape=(jax.ShapeDtyp...  54.1 us

profile of v5, /device:TPU:32, one launch (start us, length us, event | category | flops | bytes accessed | tf_op | source)
XLA Modules:
  0.0 55.5 jit_solution(7188407015226628303)
XLA Ops:
  0.6 54.1 %adapter_backward.1 = (f32[1,128,128]{2,1,0:T(8,128)S(1)}, f32[1,256,128]{2,1,0:T(8,128)S(1)}, f32[2,64,256]{2,1,0:T(8,128)S(1)}) custom-call(bf16[1,128,2048]{2,1,0:T(8,128)(2,1)} %pq_h.1, bf16[1,128,256]{2,1,0:T(8,128)(2,1)} %pk_h.1, bf16[1,128,256]{2,1,0:T(8,128)(2,1)} %pv_h.1, bf16[1,128,128]{2,1,0:T(8,128)(2,1)} %pa_h.1, bf16[1,128,2048]{2,1,0:T(8,128)(2,1)} %pg_h.1, ...), custom_call_target="tpu_custom_call" | custom-call | tf_op jit(solution)/shard_map/adapter_backward/pallas_call | solution.py:389
  54.8 0.7 %store.1 = (f32[1,128,128]{2,1,0:T(8,128)}, f32[1,256,128]{2,1,0:T(8,128)}, f32[2,64,256]{2,1,0:T(8,128)}) custom-call(f32[1,128,128]{2,1,0:T(8,128)S(1)} %get-tuple-element.6.a, f32[1,256,128]{2,1,0:T(8,128)S(1)} %get-tuple-element.7.b, f32[2,64,256]{2,1,0:T(8,128)S(1)} %get-tuple-element.8.c), custom_call_target="tpu_custom_call" | custom-call | tf_op jit(solution)/shard_map/store/pallas_call | solution.py:419

commit v6 on v5

--- a/solution.py
+++ b/solution.py
@@ -77,7 +77,7 @@
     pq_h, pk_h, pv_h, pa_h, pg_h, aq_h, ak_h, av_h, aa_h, ag_h, up_h, lens_h, pairing_h,
     prompt_out, answer_out, up_out,
     pq, pk, pv, pa, pg, aq, ak, av, aa, ag, up, lens, pairing,
-    wide_up, pack, kv_slot, pre, mid1, mid2, got, a_pre, a_cols, own_w, own_dp, own_st,
+    wide_up, pack, parcel, kv_slot, pre, pre2, mid1, mid2, got, got2, a_pre, a_cols, own_w, own_dp, own_st,
     probs_s, dsc_s, dkv, own_proj, outer_acc,
     own_half, own_twin, pre_part, pre_twin, pre_half, pre_z, pre_pick, pre_home, done_half, done_twin,
     an_send, an_recv, gr_send, gr1, gr2_send, gr2, gr3_send, gr3,
@@ -139,7 +139,10 @@
         full = (base[...].astype(jnp.float32) + lifted[:, 256 * i:256 * i + 256]).astype(jnp.bfloat16)
         for h in range(2):
             pack[16 * i + 8 * h:16 * i + 8 * h + 8] = full[:, h * HD:(h + 1) * HD].reshape(8, 16, HD)
-    pack[32:36] = pa[pl.ds(pl.multiple_of(f * 64, 64), 64), :].reshape(4, 16, HD)
+    for i, tiles in enumerate((0, 16, 8)):
+        parcel[4 * i:4 * i + 4, 0:2] = pack[tiles:tiles + 8].reshape(4, 2, 16, HD)
+    parcel[0:8, 2] = pack[24:32]
+    parcel[8:12, 2] = pa[pl.ds(pl.multiple_of(f * 64, 64), 64), :].reshape(4, 16, HD)
 
     pl.semaphore_wait(barrier, 27)
 
@@ -155,8 +158,8 @@
     for shift, k in NEAR_ORDER:
         peer_x = lax.rem(x + k, 4)
         peer = lax.rem(z_hi + SHIFTS[shift], 4) * 4 + peer_x
-        to(pack.at[pl.ds(3 * (4 * shift + peer_x), 3)], mid1.at[r], 0, {"resp": peer}).start()
-    mid1[r] = pack[pl.ds(3 * x, 3)]
+        to(parcel.at[4 * shift + peer_x], mid1.at[r], 0, {"resp": peer}).start()
+    mid1[r] = parcel[x]
     for k in range(4):
         mid1[lax.rem(z_hi + 2, 4) * 4 + k] = jnp.zeros((3, 16, HD), jnp.bfloat16)
 
@@ -197,8 +200,13 @@
     for k in RESP_ORDER:
         peer = lax.rem(r + k, N)
         mid2[peer] = mid1[held_of(peer)]
-        to(mid2.at[peer], got.at[r], 2, {"resp": peer}).start()
-    got[r] = mid1[held_of(r)]
+        to(mid2.at[peer, pl.ds(0, 2)], got.at[r], 2, {"resp": peer}).start()
+    for k in RESP_ORDER:
+        peer = lax.rem(r + k, N)
+        to(mid2.at[peer, 2], got2.at[r], 3, {"resp": peer}).start()
+    mine = mid1[held_of(r)]
+    got[r] = mine[0:2]
+    got2[r] = mine[2]
 
     own_proj[...] = mm(dkv[0:128, :], wide_up[...], NT)
     own_half[...] = own_proj[rows(1 - f, 64), :].astype(jnp.bfloat16)
@@ -236,11 +244,9 @@
                 own_st[2 * h + c, 1:2, cols] = jnp.sum(weights, axis=0, keepdims=True)
                 own_st[2 * h + c, 2:3, cols] = jnp.sum(weights * dprobs, axis=0, keepdims=True)
 
-    def slot_head(h):
+    def slot_head(h, keys, values):
         key_cols = slice(h * HD, (h + 1) * HD)
         value_cols = slice(256 + h * HD, 256 + (h + 1) * HD)
-        keys = pre[8 * h:8 * h + 8].reshape(T, HD)
-        values = pre[16 + 8 * h:24 + 8 * h].reshape(T, HD)
         key_sum, value_sum = 0.0, 0.0
         for c in range(2):
             live = row_at < lens[0, c]
@@ -267,14 +273,17 @@
     from_plane = pairing[0, r] // 4
     for shift in range(3):
         for k in range(4):
-            at = 3 * (4 * shift + k)
-            pre[at:at + 3] = got[lax.rem(from_plane + SHIFTS[shift], 4) * 4 + k]
-
-    a_pre[rows(f, 64), :] = pre[32:36].reshape(64, HD)
+            pre[4 * shift + k] = got[lax.rem(from_plane + SHIFTS[shift], 4) * 4 + k]
+    slot_head(0, pre[0:4].reshape(T, HD), pre[4:8].reshape(T, HD))
+    ready(got2.at[pl.ds(0, 15)], recv_sem.at[3])
+    for shift in range(3):
+        for k in range(4):
+            pre2[4 * shift + k] = got2[lax.rem(from_plane + SHIFTS[shift], 4) * 4 + k]
+
+    a_pre[rows(f, 64), :] = pre2[8:12].reshape(64, HD)
     a_copy = to(a_pre.at[rows(f, 64)], a_pre.at[rows(f, 64)], 5, twin)
     a_copy.start()
-    slot_head(0)
-    slot_head(1)
+    slot_head(1, pre[8:12].reshape(T, HD), pre2[0:8].reshape(T, HD))
 
     ready(a_pre.at[pl.ds(0, 64)], recv_sem.at[5])
     a_cols[:, 0:128] = jnp.transpose(a_pre[...])
@@ -359,7 +368,8 @@
         )
 
     ready(mid1.at[pl.ds(0, 11)], send_sem.at[0])
-    ready(mid2.at[pl.ds(0, 15)], send_sem.at[2])
+    ready(got.at[pl.ds(0, 15)], send_sem.at[2])
+    ready(got2.at[pl.ds(0, 15)], send_sem.at[3])
     own_copy.wait_send()
     a_copy.wait_send()
     pre_copy.wait_send()
@@ -399,8 +409,9 @@
             V((128, 2048), bf), V((128, 256), bf), V((128, 256), bf), V((128, 128), bf), V((128, 2048), bf),
             V((256, 2048), bf), V((256, 256), bf), V((256, 256), bf), V((256, 128), bf), V((256, 2048), bf),
             V((2, 64, 256), bf), pltpu.SMEM((1, 2), jnp.int32), pltpu.SMEM((1, 16), jnp.int32),
-            V((128, 512), bf), V((36, 16, 128), bf), V((256, 512), bf), V((36, 16, 128), bf),
-            V((16, 3, 16, 128), bf), V((16, 3, 16, 128), bf), V((16, 3, 16, 128), bf), V((128, 128), bf),
+            V((128, 512), bf), V((32, 16, 128), bf), V((12, 3, 16, 128), bf), V((256, 512), bf),
+            V((12, 2, 16, 128), bf), V((12, 16, 128), bf),
+            V((16, 3, 16, 128), bf), V((16, 3, 16, 128), bf), V((16, 2, 16, 128), bf), V((16, 16, 128), bf), V((128, 128), bf),
             V((128, 384), bf), V((4, 128, 1024), f32), V((4, 128, 1024), f32), V((4, 8, 1024), f32),
             V((2, 256, 1024), bf), V((2, 256, 1024), bf), V((512, 512), bf), V((128, 128), f32), V((128, 512), f32),
             V((64, 128), bf), V((64, 128), bf), V((128, 128), f32), V((64, 128), bf), V((2, 64, 128), bf),

time: 55.6 us -> 54.5 us (0.980)
  the two profiles are of different devices: /device:TPU:32 before, /device:TPU:1 now
where the time goes in v6:
time: 54.5 us; the launch traced here: 53.4 us
  Pallas kernels  52.7 us (97%)
  between operations  0.64 us (1%)
    pallas_call x1, Pallas kernels, on_device(): pl.pallas_call(functools.partial(kernel, scale), out_shape=(jax.ShapeDtyp...  52 us

profile of v6, /device:TPU:1, one launch (start us, length us, event | category | flops | bytes accessed | tf_op | source)
XLA Modules:
  0.0 53.4 jit_solution(11390340055805537793)
XLA Ops:
  0.6 52.0 %adapter_backward.1 = (f32[1,128,128]{2,1,0:T(8,128)S(1)}, f32[1,256,128]{2,1,0:T(8,128)S(1)}, f32[2,64,256]{2,1,0:T(8,128)S(1)}) custom-call(bf16[1,128,2048]{2,1,0:T(8,128)(2,1)} %pq_h.1, bf16[1,128,256]{2,1,0:T(8,128)(2,1)} %pk_h.1, bf16[1,128,256]{2,1,0:T(8,128)(2,1)} %pv_h.1, bf16[1,128,128]{2,1,0:T(8,128)(2,1)} %pa_h.1, bf16[1,128,2048]{2,1,0:T(8,128)(2,1)} %pg_h.1, ...), custom_call_target="tpu_custom_call" | custom-call | tf_op jit(solution)/shard_map/adapter_backward/pallas_call | solution.py:399
  52.6 0.7 %store.1 = (f32[1,128,128]{2,1,0:T(8,128)}, f32[1,256,128]{2,1,0:T(8,128)}, f32[2,64,256]{2,1,0:T(8,128)}) custom-call(f32[1,128,128]{2,1,0:T(8,128)S(1)} %get-tuple-element.6.a, f32[1,256,128]{2,1,0:T(8,128)S(1)} %get-tuple-element.7.b, f32[2,64,256]{2,1,0:T(8,128)S(1)} %get-tuple-element.8.c), custom_call_target="tpu_custom_call" | custom-call | tf_op jit(solution)/shard_map/store/pallas_call | solution.py:430

commit v7 on v6

--- a/solution.py
+++ b/solution.py
@@ -19,7 +19,7 @@
 EXP2_FACTOR = FACTOR * math.log2(math.e)
 SHIFTS = (0, 1, 3)
 NEAR_ORDER = ((1, 2), (2, 2), (1, 1), (2, 1), (1, 3), (2, 3), (1, 0), (2, 0), (0, 2), (0, 1), (0, 3))
-RESP_ORDER = (10, 9, 11, 8, 6, 14, 5, 7, 13, 15, 4, 12, 2, 1, 3)
+RESP_ORDER = (10, 6, 14, 9, 5, 13, 11, 7, 15, 8, 4, 12, 2, 1, 3)
 PLANE_ORDER = (10, 9, 11, 6, 14, 8, 2, 5, 7, 13, 15, 4, 12, 1, 3)
 RING_ORDER = (8, 7, 9, 6, 10, 5, 11, 4, 12, 3, 13, 2, 14, 1, 15)
 
@@ -191,20 +191,21 @@
     lax.fori_loop(0, 2, own_head, 0)
 
     loads[12].wait()
-    ready(mid1.at[pl.ds(0, 11)], recv_sem.at[0])
-
     def held_of(member):
         owner = pairing[0, member]
         return jnp.where(lax.rem(owner // 4 + 6 - z_hi, 4) == 0, r, owner)
 
-    for k in RESP_ORDER:
+    picks = [held_of(lax.rem(r + k, N)) for k in RESP_ORDER]
+    own_pick = held_of(r)
+    ready(mid1.at[pl.ds(0, 11)], recv_sem.at[0])
+    for k, pick in zip(RESP_ORDER, picks):
         peer = lax.rem(r + k, N)
-        mid2[peer] = mid1[held_of(peer)]
+        mid2[peer] = mid1[pick]
         to(mid2.at[peer, pl.ds(0, 2)], got.at[r], 2, {"resp": peer}).start()
     for k in RESP_ORDER:
         peer = lax.rem(r + k, N)
         to(mid2.at[peer, 2], got2.at[r], 3, {"resp": peer}).start()
-    mine = mid1[held_of(r)]
+    mine = mid1[own_pick]
     got[r] = mine[0:2]
     got2[r] = mine[2]
 

time: 54.5 us -> 54.2 us (level)
  no operation moved by 1% of the time
where the time goes in v7:
time: 54.2 us; the launch traced here: 53.6 us
  Pallas kernels  53 us (98%)
  between operations  0.64 us (1%)
    pallas_call x1, Pallas kernels, on_device(): pl.pallas_call(functools.partial(kernel, scale), out_shape=(jax.ShapeDtyp...  52.2 us

profile of v7, /device:TPU:1, one launch (start us, length us, event | category | flops | bytes accessed | tf_op | source)
XLA Modules:
  0.0 53.6 jit_solution(1747472475803934422)
XLA Ops:
  0.6 52.2 %adapter_backward.1 = (f32[1,128,128]{2,1,0:T(8,128)S(1)}, f32[1,256,128]{2,1,0:T(8,128)S(1)}, f32[2,64,256]{2,1,0:T(8,128)S(1)}) custom-call(bf16[1,128,2048]{2,1,0:T(8,128)(2,1)} %pq_h.1, bf16[1,128,256]{2,1,0:T(8,128)(2,1)} %pk_h.1, bf16[1,128,256]{2,1,0:T(8,128)(2,1)} %pv_h.1, bf16[1,128,128]{2,1,0:T(8,128)(2,1)} %pa_h.1, bf16[1,128,2048]{2,1,0:T(8,128)(2,1)} %pg_h.1, ...), custom_call_target="tpu_custom_call" | custom-call | tf_op jit(solution)/shard_map/adapter_backward/pallas_call | solution.py:400
  52.9 0.7 %store.1 = (f32[1,128,128]{2,1,0:T(8,128)}, f32[1,256,128]{2,1,0:T(8,128)}, f32[2,64,256]{2,1,0:T(8,128)}) custom-call(f32[1,128,128]{2,1,0:T(8,128)S(1)} %get-tuple-element.6.a, f32[1,256,128]{2,1,0:T(8,128)S(1)} %get-tuple-element.7.b, f32[2,64,256]{2,1,0:T(8,128)S(1)} %get-tuple-element.8.c), custom_call_target="tpu_custom_call" | custom-call | tf_op jit(solution)/shard_map/store/pallas_call | solution.py:431

commit v8 on v7

--- a/solution.py
+++ b/solution.py
@@ -77,7 +77,7 @@
     pq_h, pk_h, pv_h, pa_h, pg_h, aq_h, ak_h, av_h, aa_h, ag_h, up_h, lens_h, pairing_h,
     prompt_out, answer_out, up_out,
     pq, pk, pv, pa, pg, aq, ak, av, aa, ag, up, lens, pairing,
-    wide_up, pack, parcel, kv_slot, pre, pre2, mid1, mid2, got, got2, a_pre, a_cols, own_w, own_dp, own_st,
+    wide_up, pack, parcel, kv_slot, pre, pre2, mid1, mid1b, mid2, mid2b, got, got2, a_pre, a_cols, own_w, own_dp, own_st,
     probs_s, dsc_s, dkv, own_proj, outer_acc,
     own_half, own_twin, pre_part, pre_twin, pre_half, pre_z, pre_pick, pre_home, done_half, done_twin,
     an_send, an_recv, gr_send, gr1, gr2_send, gr2, gr3_send, gr3,
@@ -158,10 +158,16 @@
     for shift, k in NEAR_ORDER:
         peer_x = lax.rem(x + k, 4)
         peer = lax.rem(z_hi + SHIFTS[shift], 4) * 4 + peer_x
-        to(parcel.at[4 * shift + peer_x], mid1.at[r], 0, {"resp": peer}).start()
-    mid1[r] = parcel[x]
+        to(parcel.at[4 * shift + peer_x, pl.ds(0, 2)], mid1.at[r], 0, {"resp": peer}).start()
+    for shift, k in NEAR_ORDER:
+        peer_x = lax.rem(x + k, 4)
+        peer = lax.rem(z_hi + SHIFTS[shift], 4) * 4 + peer_x
+        to(parcel.at[4 * shift + peer_x, 2], mid1b.at[r], 1, {"resp": peer}).start()
+    mid1[r] = parcel[x, 0:2]
+    mid1b[r] = parcel[x, 2]
     for k in range(4):
-        mid1[lax.rem(z_hi + 2, 4) * 4 + k] = jnp.zeros((3, 16, HD), jnp.bfloat16)
+        mid1[lax.rem(z_hi + 2, 4) * 4 + k] = jnp.zeros((2, 16, HD), jnp.bfloat16)
+        mid1b[lax.rem(z_hi + 2, 4) * 4 + k] = jnp.zeros((16, HD), jnp.bfloat16)
 
     lane_at = lax.rem(lax.broadcasted_iota(jnp.int32, (T, 256), 1), T)
     visible = lax.broadcasted_iota(jnp.int32, (T, 256), 0) <= lane_at
@@ -201,13 +207,14 @@
     for k, pick in zip(RESP_ORDER, picks):
         peer = lax.rem(r + k, N)
         mid2[peer] = mid1[pick]
-        to(mid2.at[peer, pl.ds(0, 2)], got.at[r], 2, {"resp": peer}).start()
-    for k in RESP_ORDER:
+        to(mid2.at[peer], got.at[r], 2, {"resp": peer}).start()
+    got[r] = mid1[own_pick]
+    ready(mid1b.at[pl.ds(0, 11)], recv_sem.at[1])
+    for k, pick in zip(RESP_ORDER, picks):
         peer = lax.rem(r + k, N)
-        to(mid2.at[peer, 2], got2.at[r], 3, {"resp": peer}).start()
-    mine = mid1[own_pick]
-    got[r] = mine[0:2]
-    got2[r] = mine[2]
+        mid2b[peer] = mid1b[pick]
+        to(mid2b.at[peer], got2.at[r], 3, {"resp": peer}).start()
+    got2[r] = mid1b[own_pick]
 
     own_proj[...] = mm(dkv[0:128, :], wide_up[...], NT)
     own_half[...] = own_proj[rows(1 - f, 64), :].astype(jnp.bfloat16)
@@ -369,6 +376,7 @@
         )
 
     ready(mid1.at[pl.ds(0, 11)], send_sem.at[0])
+    ready(mid1b.at[pl.ds(0, 11)], send_sem.at[1])
     ready(got.at[pl.ds(0, 15)], send_sem.at[2])
     ready(got2.at[pl.ds(0, 15)], send_sem.at[3])
     own_copy.wait_send()
@@ -412,7 +420,8 @@
             V((2, 64, 256), bf), pltpu.SMEM((1, 2), jnp.int32), pltpu.SMEM((1, 16), jnp.int32),
             V((128, 512), bf), V((32, 16, 128), bf), V((12, 3, 16, 128), bf), V((256, 512), bf),
             V((12, 2, 16, 128), bf), V((12, 16, 128), bf),
-            V((16, 3, 16, 128), bf), V((16, 3, 16, 128), bf), V((16, 2, 16, 128), bf), V((16, 16, 128), bf), V((128, 128), bf),
+            V((16, 2, 16, 128), bf), V((16, 16, 128), bf), V((16, 2, 16, 128), bf), V((16, 16, 128), bf),
+            V((16, 2, 16, 128), bf), V((16, 16, 128), bf), V((128, 128), bf),
             V((128, 384), bf), V((4, 128, 1024), f32), V((4, 128, 1024), f32), V((4, 8, 1024), f32),
             V((2, 256, 1024), bf), V((2, 256, 1024), bf), V((512, 512), bf), V((128, 128), f32), V((128, 512), f32),
             V((64, 128), bf), V((64, 128), bf), V((128, 128), f32), V((64, 128), bf), V((2, 64, 128), bf),

time: 54.2 us -> 54.5 us (level)
    pallas_call x1, Pallas kernels: 52.2 us -> 52.8 us  [on_device(): pl.pallas_call(functools.partial(kernel, scale), out_shape=(jax.ShapeDtyp...]
where the time goes in v8:
time: 54.5 us; the launch traced here: 54.2 us
  Pallas kernels  53.5 us (98%)
  between operations  0.64 us (1%)
    pallas_call x1, Pallas kernels, on_device(): pl.pallas_call(functools.partial(kernel, scale), out_shape=(jax.ShapeDtyp...  52.8 us

profile of v8, /device:TPU:1, one launch (start us, length us, event | category | flops | bytes accessed | tf_op | source)
XLA Modules:
  0.0 54.2 jit_solution(625283411656456884)
XLA Ops:
  0.6 52.8 %adapter_backward.1 = (f32[1,128,128]{2,1,0:T(8,128)S(1)}, f32[1,256,128]{2,1,0:T(8,128)S(1)}, f32[2,64,256]{2,1,0:T(8,128)S(1)}) custom-call(bf16[1,128,2048]{2,1,0:T(8,128)(2,1)} %pq_h.1, bf16[1,128,256]{2,1,0:T(8,128)(2,1)} %pk_h.1, bf16[1,128,256]{2,1,0:T(8,128)(2,1)} %pv_h.1, bf16[1,128,128]{2,1,0:T(8,128)(2,1)} %pa_h.1, bf16[1,128,2048]{2,1,0:T(8,128)(2,1)} %pg_h.1, ...), custom_call_target="tpu_custom_call" | custom-call | tf_op jit(solution)/shard_map/adapter_backward/pallas_call | solution.py:408
  53.4 0.7 %store.1 = (f32[1,128,128]{2,1,0:T(8,128)}, f32[1,256,128]{2,1,0:T(8,128)}, f32[2,64,256]{2,1,0:T(8,128)}) custom-call(f32[1,128,128]{2,1,0:T(8,128)S(1)} %get-tuple-element.6.a, f32[1,256,128]{2,1,0:T(8,128)S(1)} %get-tuple-element.7.b, f32[2,64,256]{2,1,0:T(8,128)S(1)} %get-tuple-element.8.c), custom_call_target="tpu_custom_call" | custom-call | tf_op jit(solution)/shard_map/store/pallas_call | solution.py:440
